TPU v7x, 256 devices: a whole 4x4x8 slice. The times are simulated.
256 devices in a mesh: grp: 2 (over core), vocab: 32 (over z, y), seq: 4 (over x).
Axes of the slice: x: 4, y: 4, z: 8, core: 2. Of those that a mesh axis runs over, the one named last changes fastest.
Arguments:
- hidden_states: bfloat16 [2, 512, 4096], P('grp', 'seq'), may hold values from -6 to 6
- output_head_weights: bfloat16 [2, 4096, 114688], P('grp', None, ('vocab', 'seq')), may hold values from -0.9375 to 0.9375
- norm_gains: float32 [2, 4096], replicated, may hold values from 0.25 to 1.75
- label_ids: int32 [512], P('seq'), may hold values from 0 to 114687
Outputs:
- token_loss: float32 [512], P('seq')
- head_grad: bfloat16 [4096, 114688], P('grp', ('vocab', 'seq'))
- hidden_grad: bfloat16 [4096, 512], P(('grp', 'vocab', 'seq'))
- gain_grad: float32 [4096], P(('grp', 'vocab', 'seq'))
All inputs are finite; a program needn't handle non-finite values.
Results may differ from a plain program's by a relative error of at most 0.0091.
Values may be sent and summed in bfloat16 or wider, within the bound.
A program may use at most 128 MiB of HBM per device.

v0:
```python
import jax
import jax.numpy as jnp
from jax import lax
from jax.sharding import PartitionSpec as P

SOFTEN_TEMP = 2.0
LABEL_WEIGHT = 0.5
EPSILON = 1e-06


def from_partner(block, axis, stride):
    count = lax.axis_size(axis)
    route = []
    for low in range(count):
        high = low | 1 << stride
        if high != low and high < count:
            route += [(low, high), (high, low)]
    return lax.ppermute(block, axis, route)


def spread(value, axis, source):
    kept = jnp.where(lax.axis_index(axis) == source, value, 0).astype(value.dtype)
    return lax.psum(kept, axis)


def normalize(states, gain):
    values = states.astype(jnp.float32)
    inverse = lax.rsqrt(jnp.mean(values * values, axis=-1, keepdims=True) + EPSILON)
    unit_vals = values * inverse
    return (unit_vals, inverse, (unit_vals * gain).astype(jnp.bfloat16))


def per_device(hidden_states, output_head_weights, norm_gains, label_ids):
    own_tile = hidden_states[0]
    head_matrix = output_head_weights[0]
    model_width = head_matrix.shape[0]
    head_width = head_matrix.shape[1]
    tile_rows = own_tile.shape[0]
    group_index = lax.axis_index("grp")
    block_index = lax.axis_index(("vocab", "seq"))
    block_count = lax.axis_size(("vocab", "seq"))
    whole_vocabulary = head_width * block_count
    half_rows = model_width // 2
    shard_rows = half_rows // block_count
    is_teacher = group_index == 0
    tiles, label_all = (
        lax.all_gather(own_tile, "seq", axis=0, tiled=True),
        lax.all_gather(label_ids, "seq", axis=0, tiled=True),
    )
    own_gain = jnp.where(is_teacher, norm_gains[0], norm_gains[1])
    unit_vals, inverse, norm_applied = normalize(tiles, own_gain)
    scaled_logits = (
        jnp.dot(norm_applied, head_matrix, preferred_element_type=jnp.float32) / SOFTEN_TEMP
    )
    partner = from_partner(scaled_logits, "grp", 0)
    teacher_scaled_logits = jnp.where(is_teacher, scaled_logits, partner)
    student_scaled_logits = jnp.where(is_teacher, partner, scaled_logits)
    columns = block_index * head_width + lax.iota(jnp.int32, head_width)
    target = (columns[None, :] == label_all[:, None]).astype(jnp.float32)
    picked_part = jnp.sum(target * student_scaled_logits, axis=1)
    teacher_top, student_top = lax.pmax(
        (jnp.max(teacher_scaled_logits, axis=1), jnp.max(student_scaled_logits, axis=1)),
        ("vocab", "seq"),
    )
    teacher_exp = jnp.exp(teacher_scaled_logits - teacher_top[:, None])
    student_exp = jnp.exp(student_scaled_logits - student_top[:, None])
    teacher_total, student_total, cross_sum, picked = lax.psum(
        (
            jnp.sum(teacher_exp, axis=1),
            jnp.sum(student_exp, axis=1),
            jnp.sum(teacher_exp * (teacher_scaled_logits - student_scaled_logits), axis=1),
            picked_part,
        ),
        ("vocab", "seq"),
    )
    teacher_lse = teacher_top + jnp.log(teacher_total)
    student_lse = student_top + jnp.log(student_total)
    divergence = cross_sum / teacher_total - teacher_lse + student_lse
    loss_all = divergence + LABEL_WEIGHT * (student_lse - picked)
    teacher_prob = jnp.exp(teacher_scaled_logits - teacher_lse[:, None])
    student_prob = jnp.exp(student_scaled_logits - student_lse[:, None])
    scale_factor = whole_vocabulary / 16.0 / SOFTEN_TEMP
    logit_grad = (
        scale_factor * ((1.0 + LABEL_WEIGHT) * student_prob - teacher_prob - LABEL_WEIGHT * target)
    ).astype(jnp.bfloat16)
    contract_rows = (((0,), (0,)), ((), ()))
    row_offset = group_index * half_rows + block_index * shard_rows
    gain_rows = lax.dynamic_slice_in_dim(norm_gains[1], row_offset, shard_rows, 0)
    full_grad = lax.dot_general(
        norm_applied, logit_grad, contract_rows, preferred_element_type=jnp.float32
    ).astype(jnp.bfloat16)
    upper = lax.slice_in_dim(head_matrix, 0, shard_rows * lax.axis_size(("vocab", "seq")), axis=0)
    lower = lax.dynamic_slice_in_dim(
        head_matrix, half_rows, shard_rows * lax.axis_size(("vocab", "seq")), 0
    )
    paired = lax.psum_scatter(
        jnp.einsum(
            "rhv,tv->rht",
            jnp.stack([upper, lower], 1),
            logit_grad,
            preferred_element_type=jnp.float32,
        ),
        ("vocab", "seq"),
        scatter_dimension=0,
        tiled=True,
    )
    first_unit = lax.dynamic_slice_in_dim(unit_vals, block_index * shard_rows, shard_rows, 1).T
    given_grad = spread(full_grad[:half_rows], "grp", 1)
    given_dy, given_unit, given_inverse = (
        spread(paired[:, 0], "grp", 1),
        spread(first_unit, "grp", 1),
        spread(inverse[:, 0], "grp", 1),
    )
    second_unit = lax.dynamic_slice_in_dim(
        unit_vals, half_rows + block_index * shard_rows, shard_rows, 1
    ).T
    head_grad = jnp.where(is_teacher, given_grad, full_grad[half_rows:])
    row_grad = jnp.where(is_teacher, given_dy, paired[:, 1])
    unit_rows = jnp.where(is_teacher, given_unit, second_unit)
    inverse_row = jnp.where(is_teacher, given_inverse, inverse[:, 0])
    unit_grad = row_grad * gain_rows[:, None]
    row_total = lax.psum(jnp.sum(unit_grad * unit_rows, axis=0), ("grp", "vocab", "seq"))
    row_mean = row_total / model_width
    hidden_grad = (inverse_row[None, :] * (unit_grad - unit_rows * row_mean[None, :])).astype(
        jnp.bfloat16
    )
    gain_grad = jnp.sum(row_grad * unit_rows, axis=1)
    token_loss = lax.dynamic_slice_in_dim(loss_all, lax.axis_index("seq") * tile_rows, tile_rows, 0)
    return (token_loss, head_grad, hidden_grad, gain_grad)


def solution(mesh):
    placed = (P("grp", "seq", None), P("grp", None, ("vocab", "seq")), P(), P("seq"))
    return jax.shard_map(
        per_device,
        mesh=mesh,
        in_specs=placed,
        out_specs=(
            P("seq"),
            P("grp", ("vocab", "seq")),
            P(("grp", "vocab", "seq"), None),
            P(("grp", "vocab", "seq")),
        ),
        check_vma=False,
    )
```

profile of v0, /device:TPU:2, one launch (start us, length us, event | category | flops | bytes accessed | tf_op | source)
XLA Modules:
  0.0 1663.7 jit_solution(6158508654568807646)
XLA Ops:
  7.2 2.3 copy.9
  9.6 57.5 %all-gather.4.cloned.1.call-done = bf16[1,512,4096]{1,2,0:T(8,128)(2,1)} async-done(((bf16[1,128,4096]{1,2,0:T(8,128)(2,1)}), bf16[1,512,4096]{1,2,0:T(8,128)(2,1)}) %all-gather.4.cloned.1.call-update) | async-done | bytes 4194320 | tf_op jit(solution)/shard_map/all_gather | solution.py:47
  67.2 3.3 fusion
  71.0 7.7 fusion.12
  78.9 8.2 all-gather.1
  87.1 6.8 slice_bitcast_fusion.1
  93.9 3.7 fusion.22
  97.6 344.1 %all-reduce.1 = (f32[512]{0:T(512)S(1)}, f32[512]{0:T(512)S(1)}) all-reduce(f32[512]{0:T(512)S(1)} %get-tuple-element.26, f32[512]{0:T(512)S(1)} %get-tuple-element.30), channel_id=1, replica_groups=mesh['grp'=2,'vocab'=32,'seq'=4] {'vocab','seq'}, use_global_device_ids=true, to_apply=%region_8.9 | all-reduce | flops 1024 | bytes 8192 | tf_op jit(solution)/shard_map/pmax | solution.py:61
  441.7 2.5 multiply_reduce_fusion
  444.2 351.3 %all-reduce = (f32[512]{0:T(512)S(1)}, f32[512]{0:T(512)S(1)}, f32[512]{0:T(512)S(1)}, f32[512]{0:T(512)S(1)}) all-reduce(f32[512]{0:T(512)S(1)} %get-tuple-element.7, f32[512]{0:T(512)S(1)} %get-tuple-element.6, f32[512]{0:T(512)S(1)} %get-tuple-element.5, ...), channel_id=1, replica_groups=mesh['grp'=2,'vocab'=32,'seq'=4] {'vocab','seq'}, use_global_device_ids=true, to_apply=%region_10.11 | all-reduce | flops 2048 | bytes 16384 | tf_op jit(solution)/shard_map/psum | solution.py:67
  795.6 11.9 fusion.1
  807.5 8.0 convolution_convert_fusion
  815.6 3.0 copy-done.2
  818.5 2.1 slice_select_fusion.1
  820.8 3.4 convert_multiply_fusion
  824.2 3.2 copy-done.1
  828.6 679.6 %reduce-scatter.2.cloned.1.call-done = f32[16,2,512]{2,0,1:T(8,128)} async-done(((f32[2048,2,512]{2,0,1:T(8,128)}), f32[16,2,512]{2,0,1:T(8,128)}) %reduce-scatter.2.cloned.1.call-update) | async-done | bytes 65552 | tf_op jit(solution)/shard_map/reduce_scatter | solution.py:96
  1508.3 1.4 fusion.17
  1509.7 35.8 %all-reduce.6.cloned.1.call-done = bf16[2048,896]{1,0:T(8,128)(2,1)} async-done(((bf16[2048,896]{1,0:T(8,128)(2,1)}), bf16[2048,896]{1,0:T(8,128)(2,1)}) %all-reduce.6.cloned.1.call-update) | async-done | bytes 3670032 | tf_op jit(solution)/shard_map/psum | solution.py:23
  1545.5 5.4 slice_select_fusion
  1550.8 27.9 %all-reduce.8.cloned.1.call-done = (f32[16,512]{1,0:T(8,128)}, f32[16,512]{1,0:T(8,128)}, f32[512]{0:T(512)}) async-done(((f32[16,512]{1,0:T(8,128)}, f32[16,512]{1,0:T(8,128)}, f32[512]{0:T(512)}), (f32[16,512]{1,0:T(8,128)}, f32[16,512]{1,0:T(8,128)}, f32[512]{0:T(512)})) %all-reduce.8.cloned.1.call-update) | async-done | bytes 67600 | tf_op jit(solution)/shard_map/psum | solution.py:23
  1578.7 0.7 broadcast_select_fusion.4
  1579.4 1.5 multiply_reduce_fusion.1
  1580.9 75.6 %psum.71 = f32[512]{0:T(512)S(1)} all-reduce(f32[512]{0:T(512)S(1)} %get-tuple-element.9), channel_id=1, replica_groups=mesh['grp'=2,'vocab'=32,'seq'=4] {'grp','vocab','seq'}, use_global_device_ids=true, to_apply=%region_19.20 | all-reduce | flops 512 | bytes 4096 | tf_op jit(solution)/shard_map/psum | solution.py:122
  (31 shorter events, 2.9 us)
Async XLA Ops:
  7.2 2.4 copy-start.5
  7.2 60.0 %all-gather.4.cloned.1.call-start = ((), (), s32[]{:S(2)}) async-start(), calls=%async_computation.3 | async-start | bytes 5242880 | tf_op jit(solution)/shard_map/all_gather | solution.py:47
  9.5 1498.8 %reduce-scatter.2.cloned.1.call-start = ((), (), s32[]{:S(2)}) async-start(), calls=%async_computation.2 | async-start | bytes 8454144 | tf_op jit(solution)/shard_map/reduce_scatter | solution.py:96
  67.2 3.9 copy-start
  71.0 7.9 copy-start.6
  78.8 15.1 copy-start.3
  78.8 15.1 collective-permute-start
  807.5 738.0 %all-reduce.6.cloned.1.call-start = ((), (), s32[]{:S(2)}) async-start(), calls=%async_computation.1 | async-start | bytes 7340032 | tf_op jit(solution)/shard_map/psum | solution.py:23
  815.6 3.0 copy-start.2
  820.7 758.0 %all-reduce.8.cloned.1.call-start = ((), (), s32[]{:S(2)}) async-start(), calls=%async_computation.4 | async-start | bytes 135168 | tf_op jit(solution)/shard_map/psum | solution.py:23
  824.2 3.2 copy-start.1
  1509.6 69.7 %copy-start.4 = (f32[16,2,512]{2,0,1:T(8,128)S(1)}, f32[16,2,512]{2,0,1:T(8,128)}, u32[]{:S(2)}) copy-start(f32[16,2,512]{2,0,1:T(8,128)} %reduce-scatter.2.cloned.1.call-done) | copy-start | bytes 196612
Sparse Core Ops, SparseCore 0:
  10.4 56.7 all-gather.3
  807.6 700.6 reduce-scatter.1
  1511.6 33.7 all-reduce.5
  1548.6 30.0 all-reduce.7
where the time goes:
time: 1670 us; the launch traced here: 1660 us
  waiting for transfers between devices  801 us (48%)
  blocking collectives  779 us (47%)
  matrix products  27.6 us (2%)
  other arithmetic  25.9 us (2%)
    reduce_scatter x1, waiting for transfers between devices, per_device(): lax.psum_scatter(jnp.einsum('rhv,tv->rht', jnp.stack([upper, lower], 1),...  680 us
    psum x1, blocking collectives, per_device(): lax.psum((jnp.sum(teacher_exp, axis=1), jnp.sum(student_exp, axis=1), jnp...  351 us
    pmax x1, blocking collectives, per_device(): lax.pmax((jnp.max(teacher_scaled_logits, axis=1), jnp.max(student_scaled_...  344 us
    psum x1, blocking collectives, per_device(): lax.psum(jnp.sum(unit_grad * unit_rows, axis=0), ('grp', 'vocab', 'seq'))  75.6 us
    psum x2, waiting for transfers between devices, spread(): return lax.psum(kept, axis)  63.7 us
    all_gather x1, waiting for transfers between devices, per_device(): lax.all_gather(own_tile, 'seq', axis=0, tiled=True)  57.5 us
  transfers between devices with their start and end apart: 5, of which 4 were waited for; matrix products, arithmetic and copies ran while one was open for 2% of the time, Pallas kernels for 0%

commit v1 on v0

v1 whole, which is shorter than its diff:
```python
import jax
import jax.numpy as jnp
from jax import lax
from jax.experimental import pallas as pl
from jax.experimental.pallas import tpu as pltpu
from jax.sharding import PartitionSpec as P

SOFTEN_TEMP = 2.0
LABEL_WEIGHT = 0.5
EPSILON = 1e-06
MESH = pl.DeviceIdType.MESH
F32, BF16 = jnp.float32, jnp.bfloat16
NX, NY, NZ = 4, 4, 8
SUB = 384
Z_BASE = NY * SUB
X_BASE = 2 * NY * SUB
ROWS = 32
PEERS = [(0, 0, d) for d in (1, 2, 3)] + [(0, d, 0) for d in (1, 2, 3)] + [(d, 0, 0) for d in range(1, 8)]


def each(count, body):
    def step(i, carry):
        body(i)
        return carry

    lax.fori_loop(0, count, step, 0)


def kernel(
    hs, w_hbm, gains_hbm, label_hbm,
    loss_out, head_out, hidden_out, gain_out,
    xg, nrm, w, w1h, n1h, n1t, z, zp, e0s, e1s, z1s, lg,
    info, info1, invb, labb, gains, label, xblk, ut,
    statc, st_send, st_recv, lossrt, colb,
    ng, r1, s2, r2, s3, r3, rt_s, rt_r1, rt_r2, rt_r3, fin, hg,
    loc, xs_s, xs_r, ys_s, ys_r, zs_s, zs_r, in_s, in_r, pr_s, pr_r,
    sa_s, sa_r, sz_s, sz_r, ab_s, ab_r, cz_s, cz_r, hg_s,
):
    g = lax.axis_index("grp")
    v = lax.axis_index("vocab")
    s = lax.axis_index("seq")
    zc = lax.div(v, NY)
    yc = lax.rem(v, NY)
    other = 1 - g
    is_teacher = g == 0

    def device(dz, dy, dx):
        return {
            "grp": g,
            "vocab": lax.rem(zc + dz, NZ) * NY + lax.rem(yc + dy, NY),
            "seq": lax.rem(s + dx, NX),
        }

    partner = {"grp": other, "vocab": v, "seq": s}

    def remote(src, dst, ssem, rsem, to):
        return pltpu.make_async_remote_copy(
            src_ref=src, dst_ref=dst, send_sem=ssem, recv_sem=rsem, device_id=to, device_id_type=MESH
        )

    load_x = pltpu.make_async_copy(hs.at[0], xg.at[s], loc.at[0])
    load_g = pltpu.make_async_copy(gains_hbm, gains, loc.at[1])
    load_l = pltpu.make_async_copy(label_hbm, label, loc.at[2])
    load_w = pltpu.make_async_copy(w_hbm.at[0], w, loc.at[3])
    load_x.start()
    load_g.start()
    load_l.start()
    load_w.start()

    barrier = pltpu.get_barrier_semaphore()
    for dz, dy, dx in PEERS:
        pl.semaphore_signal(barrier, inc=1, device_id=device(dz, dy, dx), device_id_type=MESH)
    pl.semaphore_signal(barrier, inc=1, device_id=partner, device_id_type=MESH)
    pl.semaphore_wait(barrier, len(PEERS) + 1)

    zf = lax.div(zc, 2)
    zh = lax.rem(zc, 2)

    def y_cols(y):
        return pl.ds(pl.multiple_of(y * SUB, 128), SUB)

    def z_cols(f):
        return pl.ds(pl.multiple_of(Z_BASE + f * SUB, 128), SUB)

    x_cols = pl.ds(X_BASE, 4096 - X_BASE)

    def z_rows(h):
        return pl.ds(pl.multiple_of(h * 64, 64), 64)

    def x_copy(kind, d, to):
        if kind == 0:
            rows, cols = pl.ds(0, 128), y_cols(yc)
        elif kind == 1:
            rows, cols = z_rows(zh), z_cols(zf)
        else:
            rows, cols = pl.ds(0, 128), x_cols
        at = s if to else lax.rem(s + NX - d, NX)
        dst = xg.at[at, rows, cols]
        return remote(
            hs.at[0, rows, cols] if to else dst, dst, xs_s.at[kind, d - 1], xs_r.at[kind, d - 1], device(0, 0, d)
        )

    for kind in range(3):
        each(3, lambda i, kind=kind: x_copy(kind, i + 1, True).start())

    half_w = pl.ds(0, 2048)

    def w_copy():
        return remote(w_hbm.at[0, half_w, :], w1h, pr_s.at[0], pr_r.at[0], partner)

    load_w1 = pltpu.make_async_copy(w_hbm.at[0, pl.ds(2048, 2048), :], w1h, loc.at[4])

    @pl.when(g == 1)
    def _():
        w_copy().start()
        load_w1.start()

    load_x.wait()
    load_g.wait()
    load_l.wait()
    total = jnp.zeros((128, 128), F32)
    for b in range(32):
        part = xg[s, :, pl.ds(b * 128, 128)].astype(F32)
        total += part * part
    mean = jnp.sum(total, axis=1, keepdims=True) * (1.0 / 4096)
    inverse = lax.rsqrt(mean + EPSILON)
    inverse_rows = jnp.transpose(jnp.broadcast_to(inverse, (128, 128)))[0:8]
    sub8 = lax.broadcasted_iota(jnp.int32, (8, 128), 0)
    label_rows = jnp.broadcast_to(label[...].astype(F32), (8, 128))
    info[s] = jnp.where(sub8 == 1, label_rows, inverse_rows)

    def info_copy(d, to):
        at = s if to else lax.rem(s + NX - d, NX)
        return remote(info.at[at], info.at[at], in_s.at[d - 1], in_r.at[d - 1], device(0, 0, d))

    each(3, lambda i: info_copy(i + 1, True).start())

    def y_copy(dy, d, to):
        shard = lax.rem(s + NX - d, NX)
        y = yc if to else lax.rem(yc + NY - dy, NY)
        ref = xg.at[shard, :, y_cols(y)]
        return remote(ref, ref, ys_s.at[dy - 1, d - 1], ys_r.at[dy - 1, d - 1], device(0, dy, 0))

    def z_copy(dz, d, to):
        shard = lax.rem(s + NX - d, NX)
        at = zc if to else lax.rem(zc + NZ - dz, NZ)
        ref = xg.at[shard, z_rows(lax.rem(at, 2)), z_cols(lax.div(at, 2))]
        return remote(ref, ref, zs_s.at[dz - 1, d - 1], zs_r.at[dz - 1, d - 1], device(dz, 0, 0))

    def forward_y(i):
        x_copy(0, i + 1, False).wait_recv()
        each(3, lambda j: y_copy(j + 1, i + 1, True).start())

    def forward_z(i):
        x_copy(1, i + 1, False).wait_recv()
        each(7, lambda j: z_copy(j + 1, i + 1, True).start())

    each(3, forward_y)
    each(3, forward_z)

    each(3, lambda i: info_copy(i + 1, False).wait_recv())
    tall = jnp.transpose(jnp.concatenate([info[i] for i in range(4)] + [jnp.zeros((96, 128), F32)], axis=0))
    for i in range(4):
        invb[i] = jnp.broadcast_to(tall[:, 8 * i : 8 * i + 1], (128, 128))
        labb[pl.ds(128 * i, 128), :] = jnp.broadcast_to(tall[:, 8 * i + 1 : 8 * i + 2], (128, 128))
    load_w.wait()

    def accumulate(f0, width, first=False):
        for b in range(width // 128):
            cols = pl.ds(pl.multiple_of(f0 + b * 128, 128), 128)
            gain = jnp.where(is_teacher, gains[0:1, cols], gains[1:2, cols])
            for i in range(4):
                unit = xg[i, :, cols].astype(F32) * invb[i]
                nrm[pl.ds(i * 128, 128), cols] = (unit * gain).astype(BF16)
        cols = pl.ds(pl.multiple_of(f0, 128), width)
        product = jnp.dot(nrm[:, cols], w[cols, :], preferred_element_type=F32)
        if first:
            z[...] = product
        else:
            z[...] += product

    accumulate(yc * SUB, SUB, first=True)

    def take_y(i):
        each(3, lambda j: y_copy(i + 1, j + 1, False).wait_recv())
        accumulate(lax.rem(yc + NY - (i + 1), NY) * SUB, SUB)

    each(3, take_y)

    each(3, lambda i: x_copy(2, i + 1, False).wait_recv())
    accumulate(X_BASE, 512)
    accumulate(X_BASE + 512, 512)

    def take_z(dz):
        each(3, lambda j: z_copy(dz, j + 1, False).wait_recv())

    each(7, lambda j: take_z(j + 1))
    each(4, lambda i: accumulate(Z_BASE + i * SUB, SUB))

    own = pl.ds(pl.multiple_of(g * 256, 256), 256)
    theirs = pl.ds(pl.multiple_of(other * 256, 256), 256)
    z_trade = remote(z.at[theirs, :], zp, pr_s.at[1], pr_r.at[1], partner)
    z_trade.start()

    vs = v * NX + s
    teacher_block = lax.div(vs, 8)
    block = g * 16 + teacher_block

    def block_cols(b):
        return pl.ds(pl.multiple_of(b * 128, 128), 128)

    xblk_copy = remote(xg.at[:, :, block_cols(teacher_block)], xblk, pr_s.at[2], pr_r.at[2], partner)
    info_pair = remote(info, info1, pr_s.at[3], pr_r.at[3], partner)
    n1_copy = remote(nrm.at[:, half_w], n1h, pr_s.at[4], pr_r.at[4], partner)
    own_block = pltpu.make_async_copy(xg.at[:, :, block_cols(block)], xblk, loc.at[5])
    own_info = pltpu.make_async_copy(info, info1, loc.at[6])
    own_n1 = pltpu.make_async_copy(nrm.at[:, pl.ds(2048, 2048)], n1h, loc.at[7])

    @pl.when(g == 1)
    def _():
        xblk_copy.start()
        info_pair.start()
        n1_copy.start()
        own_block.start()
        own_info.start()
        own_n1.start()

    z_trade.wait_recv()

    lane = lax.broadcasted_iota(jnp.int32, (ROWS, 128), 1)
    column = lax.broadcasted_iota(jnp.int32, (ROWS, 896), 1)

    def labels_at(r):
        rows = pl.ds(pl.multiple_of(g * 256 + r * ROWS, ROWS), ROWS)
        return labb[rows, 0:1].astype(jnp.int32) - vs * 896

    def totals(r):
        rows = pl.ds(pl.multiple_of(r * ROWS, ROWS), ROWS)
        mine = z[pl.ds(pl.multiple_of(g * 256 + r * ROWS, ROWS), ROWS), :] * (1.0 / SOFTEN_TEMP)
        given = zp[rows, :] * (1.0 / SOFTEN_TEMP)
        z0 = jnp.where(is_teacher, mine, given)
        z1 = jnp.where(is_teacher, given, mine)
        m0 = jnp.max(z0, axis=1, keepdims=True)
        m1 = jnp.max(z1, axis=1, keepdims=True)
        e0 = jnp.exp(z0 - m0)
        e1 = jnp.exp(z1 - m1)
        e0s[rows, :] = e0
        e1s[rows, :] = e1
        z1s[rows, :] = z1
        t0 = jnp.sum(e0, axis=1, keepdims=True)
        t1 = jnp.sum(e1, axis=1, keepdims=True)
        cross = jnp.sum(e0 * (z0 - z1), axis=1, keepdims=True)
        picked = jnp.sum(jnp.where(column == labels_at(r), z1, 0.0), axis=1, keepdims=True)
        stats = jnp.zeros((ROWS, 128), F32)
        for i, value in enumerate((m0, t0, cross, m1, t1, picked)):
            stats = jnp.where(lane == i, value, stats)
        statc[rows, :] = stats

    each(256 // ROWS, totals)
    local = jnp.transpose(statc[...])[0:8]
    st_send[0] = local

    def merge(parts):
        m0 = parts[0][0:1]
        m1 = parts[0][3:4]
        for p in parts[1:]:
            m0 = jnp.maximum(m0, p[0:1])
            m1 = jnp.maximum(m1, p[3:4])
        t0 = cross = t1 = picked = jnp.zeros((1, 256), F32)
        for p in parts:
            s0 = jnp.exp(p[0:1] - m0)
            s1 = jnp.exp(p[3:4] - m1)
            t0 += s0 * p[1:2]
            cross += s0 * p[2:3]
            t1 += s1 * p[4:5]
            picked += p[5:6]
        return jnp.concatenate([m0, t0, cross, m1, t1, picked, picked, picked], axis=0)

    def st_copy(axis, d):
        to = device(0, 0, d) if axis == 0 else device(0, d, 0) if axis == 1 else device(d, 0, 0)
        sems = (sz_s.at[d - 1], sz_r.at[d - 1]) if axis == 2 else (sa_s.at[axis, d - 1], sa_r.at[axis, d - 1])
        return remote(st_send.at[axis], st_recv.at[axis * 3 + d - 1], *sems, to)

    merged = local
    for axis, count in ((0, 3), (1, 3), (2, 7)):
        if axis:
            st_send[axis] = merged
        each(count, lambda i, axis=axis: st_copy(axis, i + 1).start())
        each(count, lambda i, axis=axis: st_copy(axis, i + 1).wait_recv())
        merged = merge([merged] + [st_recv[axis * 3 + i] for i in range(count)])

    lse0 = merged[0:1] + jnp.log(merged[1:2])
    lse1 = merged[3:4] + jnp.log(merged[4:5])
    loss = merged[2:3] / merged[1:2] - lse0 + lse1 + LABEL_WEIGHT * (lse1 - merged[5:6])
    scale = 128 * 896 / 16.0 / SOFTEN_TEMP
    a0 = scale * jnp.exp(local[0:1] - lse0)
    a1 = (scale * (1.0 + LABEL_WEIGHT)) * jnp.exp(local[3:4] - lse1)
    colb[...] = jnp.transpose(jnp.concatenate([a0, a1, jnp.zeros((126, 256), F32)], axis=0))

    def gradient(r):
        rows = pl.ds(pl.multiple_of(r * ROWS, ROWS), ROWS)
        cols = colb[rows, :]
        target = jnp.where(column == labels_at(r), scale * LABEL_WEIGHT, 0.0)
        grad = (cols[:, 1:2] * e1s[rows, :] - cols[:, 0:1] * e0s[rows, :] - target).astype(BF16)
        lg[pl.ds(pl.multiple_of(g * 256 + r * ROWS, ROWS), ROWS), :] = grad
        along = jnp.sum(grad.astype(F32) * z1s[rows, :], axis=1, keepdims=True)
        statc[rows, :] = jnp.broadcast_to(along, (ROWS, 128))

    each(256 // ROWS, gradient)
    lg_trade = remote(lg.at[own, :], lg.at[own, :], pr_s.at[5], pr_r.at[5], partner)
    lg_trade.start()
    along_row = jnp.transpose(statc[...])[0:8]
    sub8w = lax.broadcasted_iota(jnp.int32, (8, 256), 0)
    lossrt[g] = jnp.where(sub8w == 0, jnp.broadcast_to(loss, (8, 256)), along_row)
    rt_trade = remote(lossrt.at[g], lossrt.at[g], pr_s.at[6], pr_r.at[6], partner)
    rt_trade.start()

    @pl.when(g == 0)
    def _():
        w_copy().wait_recv()

    @pl.when(g == 1)
    def _():
        load_w1.wait()

    def states_grad(h):
        tokens = lg[pl.ds(pl.multiple_of(h * 256, 256), 256), :]

        def tile(i):
            rows = w1h[pl.ds(pl.multiple_of(i * 512, 512), 512), :]
            product = lax.dot_general(rows, tokens, (((1,), (1,)), ((), ())), preferred_element_type=F32)
            for k in range(2):
                for y in range(NY):
                    for x in range(NX):
                        at = k * 256 + (y * NX + x) * 16
                        a = x + (y - x) * h
                        b = y + (x - y) * h
                        ng[h, a, b, 2 * i + k] = product[at : at + 16].astype(BF16)

        each(4, tile)

    def first(h):
        return s + (yc - s) * h

    def second(h):
        return yc + (s - yc) * h

    def a_copy(h, d):
        to = device(0, d * h, d * (1 - h))
        return remote(ng.at[h, lax.rem(first(h) + d, 4)], r1.at[h, d - 1], ab_s.at[h, 0, d - 1], ab_r.at[h, 0, d - 1], to)

    def at_copy(h, d):
        to = device(0, d * h, d * (1 - h))
        return remote(lossrt.at[h], rt_r1.at[h, d - 1], ab_s.at[h, 1, d - 1], ab_r.at[h, 1, d - 1], to)

    def b_copy(h, d):
        to = device(0, d * (1 - h), d * h)
        return remote(s2.at[h, lax.rem(second(h) + d, 4)], r2.at[h, d - 1], ab_s.at[h, 2, d - 1], ab_r.at[h, 2, d - 1], to)

    def bt_copy(h, d):
        to = device(0, d * (1 - h), d * h)
        return remote(rt_s.at[h, 0], rt_r2.at[h, d - 1], ab_s.at[h, 3, d - 1], ab_r.at[h, 3, d - 1], to)

    def c_copy(h, d):
        return remote(s3.at[h, lax.rem(zc + d, NZ)], r3.at[h, d - 1], cz_s.at[h, 0, d - 1], cz_r.at[h, 0, d - 1], device(d, 0, 0))

    def ct_copy(h, d):
        return remote(rt_s.at[h, 1], rt_r3.at[h, d - 1], cz_s.at[h, 1, d - 1], cz_r.at[h, 1, d - 1], device(d, 0, 0))

    def start_a(h):
        def go(i):
            a_copy(h, i + 1).start()
            at_copy(h, i + 1).start()

        each(3, go)

    def start_b(h):
        def got(i):
            a_copy(h, i + 1).wait_recv()
            at_copy(h, i + 1).wait_recv()

        each(3, got)
        mine = first(h)

        def add(b):
            for k in range(NZ):
                total = ng[h, mine, b, k].astype(F32)
                for i in range(3):
                    total += r1[h, i, b, k].astype(F32)
                s2[h, b, k] = total.astype(BF16)

        each(4, add)
        rt_s[h, 0] = lossrt[h] + rt_r1[h, 0] + rt_r1[h, 1] + rt_r1[h, 2]

        def go(i):
            b_copy(h, i + 1).start()
            bt_copy(h, i + 1).start()

        each(3, go)

    def start_c(h):
        def got(i):
            b_copy(h, i + 1).wait_recv()
            bt_copy(h, i + 1).wait_recv()

        each(3, got)
        mine = second(h)
        for k in range(NZ):
            total = s2[h, mine, k].astype(F32)
            for i in range(3):
                total += r2[h, i, k].astype(F32)
            s3[h, k] = total.astype(BF16)
        rt_s[h, 1] = rt_s[h, 0] + rt_r2[h, 0] + rt_r2[h, 1] + rt_r2[h, 2]

        def go(i):
            c_copy(h, i + 1).start()
            ct_copy(h, i + 1).start()

        each(7, go)

    def finish(h):
        def got(i):
            c_copy(h, i + 1).wait_recv()
            ct_copy(h, i + 1).wait_recv()

        each(7, got)
        total = s3[h, zc].astype(F32)
        along = rt_s[h, 1]
        for i in range(7):
            total += r3[h, i].astype(F32)
            along += rt_r3[h, i]
        fin[h] = total
        rt_s[h, 2] = along

    states_grad(g)
    start_a(g)
    lg_trade.wait()
    rt_trade.wait()
    states_grad(other)
    start_a(other)

    @pl.when(g == 0)
    def _():
        n1_copy.wait_recv()
        xblk_copy.wait_recv()
        info_pair.wait_recv()

    @pl.when(g == 1)
    def _():
        own_n1.wait()
        own_block.wait()
        own_info.wait()

    def flip(i):
        cols = pl.ds(pl.multiple_of(i * 128, 128), 128)
        n1t[cols, :] = jnp.transpose(n1h[:, cols])

    each(16, flip)

    def head_store(i):
        rows = pl.ds(pl.multiple_of(i * 512, 512), 512)
        return pltpu.make_async_copy(hg.at[rows, :], head_out.at[rows, :], hg_s.at[i])

    def head_tile(i):
        rows = pl.ds(pl.multiple_of(i * 512, 512), 512)
        hg[rows, :] = jnp.dot(n1t[rows, :], lg[...], preferred_element_type=F32).astype(BF16)
        head_store(i).start()

    each(4, head_tile)

    inv_row = jnp.concatenate([info1[i, 0:1] for i in range(4)], axis=1)
    for i in range(4):
        unit = jnp.transpose(xblk[i].astype(F32)) * info1[i, 0:1]
        ut[:, pl.ds(i * 128, 128)] = unit
    gain_col = jnp.transpose(jnp.broadcast_to(gains[1:2, block_cols(block)], (128, 128)))
    statc[pl.ds(0, 128), :] = gain_col

    start_b(g)
    start_b(other)
    start_c(g)
    start_c(other)
    finish(g)
    finish(other)

    mine16 = pl.ds(pl.multiple_of(lax.rem(vs, 8) * 16, 16), 16)
    gain16 = statc[mine16, 0:1]
    gain_total = jnp.zeros((16, 1), F32)
    for h in range(2):
        cols = pl.ds(h * 256, 256)
        unit = ut[mine16, cols]
        grad = fin[h]
        row_mean = rt_s[h, 2][1:2] * (SOFTEN_TEMP / 4096)
        hidden = inv_row[:, h * 256 : h * 256 + 256] * (grad * gain16 - unit * row_mean)
        hidden_out[:, cols] = hidden.astype(BF16)
        gain_total += jnp.sum(grad * unit, axis=1, keepdims=True)
    wide = jnp.concatenate([jnp.broadcast_to(gain_total, (16, 128)), jnp.zeros((112, 128), F32)], axis=0)
    gain_out[...] = jnp.transpose(wide)[0:1]
    loss_out[...] = lossrt[lax.div(s, 2), 0:1, pl.ds(pl.multiple_of(lax.rem(s, 2) * 128, 128), 128)]

    for kind in range(3):
        each(3, lambda i, kind=kind: x_copy(kind, i + 1, True).wait_send())

    def sent_yz(i):
        info_copy(i + 1, True).wait_send()
        each(3, lambda j: y_copy(j + 1, i + 1, True).wait_send())
        each(7, lambda j: z_copy(j + 1, i + 1, True).wait_send())

    each(3, sent_yz)
    z_trade.wait_send()

    @pl.when(g == 1)
    def _():
        w_copy().wait_send()
        xblk_copy.wait_send()
        info_pair.wait_send()
        n1_copy.wait_send()

    for axis, count in ((0, 3), (1, 3), (2, 7)):
        each(count, lambda i, axis=axis: st_copy(axis, i + 1).wait_send())

    def sent_ab(h):
        def one(i):
            a_copy(h, i + 1).wait_send()
            at_copy(h, i + 1).wait_send()
            b_copy(h, i + 1).wait_send()
            bt_copy(h, i + 1).wait_send()

        def two(i):
            c_copy(h, i + 1).wait_send()
            ct_copy(h, i + 1).wait_send()

        each(3, one)
        each(7, two)

    each(2, sent_ab)
    each(4, lambda i: head_store(i).wait())


def per_device(hidden_states, output_head_weights, norm_gains, label_ids):
    dma = pltpu.SemaphoreType.DMA
    vm = pltpu.VMEM
    scratch = [
        vm((4, 128, 4096), BF16),
        vm((512, 4096), BF16),
        vm((4096, 896), BF16),
        vm((2048, 896), BF16),
        vm((512, 2048), BF16),
        vm((2048, 512), BF16),
        vm((512, 896), F32),
        vm((256, 896), F32),
        vm((256, 896), F32),
        vm((256, 896), F32),
        vm((256, 896), F32),
        vm((512, 896), BF16),
        vm((4, 8, 128), F32),
        vm((4, 8, 128), F32),
        vm((4, 128, 128), F32),
        vm((512, 128), F32),
        vm((2, 4096), F32),
        vm((1, 128), jnp.int32),
        vm((4, 128, 128), BF16),
        vm((128, 512), F32),
        vm((256, 128), F32),
        vm((3, 8, 256), F32),
        vm((13, 8, 256), F32),
        vm((2, 8, 256), F32),
        vm((256, 128), F32),
        vm((2, 4, 4, 8, 16, 256), BF16),
        vm((2, 3, 4, 8, 16, 256), BF16),
        vm((2, 4, 8, 16, 256), BF16),
        vm((2, 3, 8, 16, 256), BF16),
        vm((2, 8, 16, 256), BF16),
        vm((2, 7, 16, 256), BF16),
        vm((2, 3, 8, 256), F32),
        vm((2, 3, 8, 256), F32),
        vm((2, 3, 8, 256), F32),
        vm((2, 7, 8, 256), F32),
        vm((2, 16, 256), F32),
        vm((2048, 896), BF16),
        dma((8,)),
        dma((3, 3)), dma((3, 3)),
        dma((3, 3)), dma((3, 3)),
        dma((7, 3)), dma((7, 3)),
        dma((3,)), dma((3,)),
        dma((7,)), dma((7,)),
        dma((2, 3)), dma((2, 3)),
        dma((7,)), dma((7,)),
        dma((2, 4, 3)), dma((2, 4, 3)),
        dma((2, 2, 7)), dma((2, 2, 7)),
        dma((4,)),
    ]
    whole = pl.BlockSpec(memory_space=pl.ANY)
    vmem = pl.BlockSpec(memory_space=pltpu.VMEM)
    loss, head_grad, hidden_grad, gain_grad = pl.pallas_call(
        kernel,
        name="distill",
        out_shape=(
            jax.ShapeDtypeStruct((1, 128), F32),
            jax.ShapeDtypeStruct((2048, 896), BF16),
            jax.ShapeDtypeStruct((16, 512), BF16),
            jax.ShapeDtypeStruct((1, 128), F32),
        ),
        in_specs=[whole] * 4,
        out_specs=(vmem, whole, vmem, vmem),
        scratch_shapes=scratch,
        cost_estimate=pl.CostEstimate(flops=10**10, bytes_accessed=2 * 10**7, transcendentals=10**6),
        compiler_params=pltpu.CompilerParams(
            collective_id=0, has_side_effects=True, vmem_limit_bytes=60 * 2**20
        ),
    )(hidden_states, output_head_weights, norm_gains, label_ids.reshape(1, 128))
    return loss.reshape(128), head_grad, hidden_grad, gain_grad[0, :16]


def solution(mesh):
    placed = (P("grp", "seq", None), P("grp", None, ("vocab", "seq")), P(), P("seq"))
    return jax.shard_map(
        per_device,
        mesh=mesh,
        in_specs=placed,
        out_specs=(
            P("seq"),
            P("grp", ("vocab", "seq")),
            P(("grp", "vocab", "seq"), None),
            P(("grp", "vocab", "seq")),
        ),
        check_vma=False,
    )
```

time: 1670 us -> 104 us (0.06)
  waiting for transfers between devices: 801 us -> 0 us
  blocking collectives: 779 us -> 0 us
  Pallas kernels: 0 us -> 95.7 us
  matrix products: 27.6 us -> 0 us
  other arithmetic: 25.9 us -> 0 us
    reduce_scatter x1 -> x0, waiting for transfers between devices: 680 us -> none  [per_device(): lax.psum_scatter(jnp.einsum('rhv,tv->rht', jnp.stack([upper, lower], 1),...]
    psum x2 -> x0, blocking collectives: 427 us -> none  [the longest x1 351 us: per_device(): lax.psum((jnp.sum(teacher_exp, axis=1), jnp.sum(student_exp, axis=1), jnp...]
    pmax x1 -> x0, blocking collectives: 344 us -> none  [per_device(): lax.pmax((jnp.max(teacher_scaled_logits, axis=1), jnp.max(student_scaled_...]
    pallas_call x0 -> x1, Pallas kernels: none -> 95.7 us  [per_device(): pl.pallas_call(kernel, name='distill', out_shape=(jax.ShapeDtypeStruct((1...]
    psum x2 -> x0, waiting for transfers between devices: 63.7 us -> none  [spread(): return lax.psum(kept, axis)]
    all_gather x1 -> x0, waiting for transfers between devices: 57.5 us -> none  [per_device(): lax.all_gather(own_tile, 'seq', axis=0, tiled=True)]
    dot_general x3 -> x0, matrix products: 27.6 us -> none  [the longest x1 11.9 us: per_device(): jnp.einsum('rhv,tv->rht', jnp.stack([upper, lower], 1), logit_grad, prefe...]
  transfers between devices with their start and end apart: 5 -> 0, of which waited for: 4 -> 0; matrix products, arithmetic and copies ran while one was open for 2% -> 0% of each run, Pallas kernels for 0% -> 0%
where the time goes in v1:
time: 104 us; the launch traced here: 103 us
  Pallas kernels  95.7 us (92%)
  local copies, waits for them, and re-layouts  7.08 us (7%)
    pallas_call x1, Pallas kernels, per_device(): pl.pallas_call(kernel, name='distill', out_shape=(jax.ShapeDtypeStruct((1...  95.7 us
    unnamed x5, local copies, waits for them, and re-layouts  5.9 us

profile of v1, /device:TPU:2, one launch (start us, length us, event | category | flops | bytes accessed | tf_op | source)
XLA Modules:
  0.0 103.4 jit_solution(6917465154204099425)
XLA Ops:
  0.6 95.7 %distill.1 = (f32[1,128]{1,0:T(1,128)}, bf16[2048,896]{1,0:T(8,128)(2,1)}, bf16[16,512]{1,0:T(8,128)(2,1)}, f32[1,128]{1,0:T(1,128)}) custom-call(bf16[1,128,4096]{2,1,0:T(8,128)(2,1)} %hs.1, bf16[1,4096,896]{2,1,0:T(8,128)(2,1)} %w_hbm.1, f32[2,4096]{1,0:T(2,128)} %gains_hbm.1, s32[1,128]{1,0:T(1,128)} %bitcast.4), custom_call_target="tpu_custom_call" | custom-call | flops 10000000000 | bytes 20000000 | tf_op jit(solution)/shard_map/distill/pallas_call | solution.py:594
  96.3 1.2 %slice_bitcast_fusion = f32[16]{0:T(128)} fusion(f32[1,128]{1,0:T(1,128)} %get-tuple-element.11), kind=kLoop, calls=%fused_computation | loop fusion | bytes 128 | tf_op jit(solution)/shard_map/squeeze | solution.py:611
  97.5 1.1 %copy.11 = f32[128]{0:T(128)} copy(f32[128]{0:T(128)} %bitcast.5) | data formatting | bytes 1024
  98.6 0.0 copy-start
  98.6 4.2 %copy.12 = bf16[2048,896]{1,0:T(8,128)(2,1)} copy(bf16[2048,896]{1,0:T(8,128)(2,1)} %get-tuple-element.17) | data formatting | bytes 7340032
  102.8 0.0 copy-done
  102.8 0.6 copy.13
Async XLA Ops:
  98.6 4.2 %copy-start = (bf16[16,512]{1,0:T(8,128)(2,1)S(1)}, bf16[16,512]{1,0:T(8,128)(2,1)}, u32[]{:S(2)}) copy-start(bf16[16,512]{1,0:T(8,128)(2,1)} %get-tuple-element.18) | copy-start | bytes 49156

commit v2 on v1

--- a/solution.py
+++ b/solution.py
@@ -11,9 +11,9 @@
 MESH = pl.DeviceIdType.MESH
 F32, BF16 = jnp.float32, jnp.bfloat16
 NX, NY, NZ = 4, 4, 8
-SUB = 384
-Z_BASE = NY * SUB
-X_BASE = 2 * NY * SUB
+Y_SUB, Z_SUB = 512, 128
+Z_BASE = NY * Y_SUB
+X_BASE = Z_BASE + NZ * Z_SUB
 ROWS = 32
 PEERS = [(0, 0, d) for d in (1, 2, 3)] + [(0, d, 0) for d in (1, 2, 3)] + [(d, 0, 0) for d in range(1, 8)]
 
@@ -32,9 +32,9 @@
     xg, nrm, w, w1h, n1h, n1t, z, zp, e0s, e1s, z1s, lg,
     info, info1, invb, labb, gains, label, xblk, ut,
     statc, st_send, st_recv, lossrt, colb,
-    ng, r1, s2, r2, s3, r3, rt_s, rt_r1, rt_r2, rt_r3, fin, hg,
+    ng, q1, q2, r1, s2, r2, s3, r3, rt_s, rt_r1, rt_r2, rt_r3, fin,
     loc, xs_s, xs_r, ys_s, ys_r, zs_s, zs_r, in_s, in_r, pr_s, pr_r,
-    sa_s, sa_r, sz_s, sz_r, ab_s, ab_r, cz_s, cz_r, hg_s,
+    sa_s, sa_r, sz_s, sz_r, ab_s, ab_r, cz_s, cz_r,
 ):
     g = lax.axis_index("grp")
     v = lax.axis_index("vocab")
@@ -71,50 +71,6 @@
     for dz, dy, dx in PEERS:
         pl.semaphore_signal(barrier, inc=1, device_id=device(dz, dy, dx), device_id_type=MESH)
     pl.semaphore_signal(barrier, inc=1, device_id=partner, device_id_type=MESH)
-    pl.semaphore_wait(barrier, len(PEERS) + 1)
-
-    zf = lax.div(zc, 2)
-    zh = lax.rem(zc, 2)
-
-    def y_cols(y):
-        return pl.ds(pl.multiple_of(y * SUB, 128), SUB)
-
-    def z_cols(f):
-        return pl.ds(pl.multiple_of(Z_BASE + f * SUB, 128), SUB)
-
-    x_cols = pl.ds(X_BASE, 4096 - X_BASE)
-
-    def z_rows(h):
-        return pl.ds(pl.multiple_of(h * 64, 64), 64)
-
-    def x_copy(kind, d, to):
-        if kind == 0:
-            rows, cols = pl.ds(0, 128), y_cols(yc)
-        elif kind == 1:
-            rows, cols = z_rows(zh), z_cols(zf)
-        else:
-            rows, cols = pl.ds(0, 128), x_cols
-        at = s if to else lax.rem(s + NX - d, NX)
-        dst = xg.at[at, rows, cols]
-        return remote(
-            hs.at[0, rows, cols] if to else dst, dst, xs_s.at[kind, d - 1], xs_r.at[kind, d - 1], device(0, 0, d)
-        )
-
-    for kind in range(3):
-        each(3, lambda i, kind=kind: x_copy(kind, i + 1, True).start())
-
-    half_w = pl.ds(0, 2048)
-
-    def w_copy():
-        return remote(w_hbm.at[0, half_w, :], w1h, pr_s.at[0], pr_r.at[0], partner)
-
-    load_w1 = pltpu.make_async_copy(w_hbm.at[0, pl.ds(2048, 2048), :], w1h, loc.at[4])
-
-    @pl.when(g == 1)
-    def _():
-        w_copy().start()
-        load_w1.start()
-
     load_x.wait()
     load_g.wait()
     load_l.wait()
@@ -129,34 +85,77 @@
     label_rows = jnp.broadcast_to(label[...].astype(F32), (8, 128))
     info[s] = jnp.where(sub8 == 1, label_rows, inverse_rows)
 
+    pl.semaphore_wait(barrier, len(PEERS) + 1)
+
+    def y_cols(y):
+        return pl.ds(pl.multiple_of(y * Y_SUB, 128), Y_SUB)
+
+    def y_half(y, k):
+        return pl.ds(pl.multiple_of(y * Y_SUB + k * (Y_SUB // 2), 128), Y_SUB // 2)
+
+    def z_cols(at):
+        return pl.ds(pl.multiple_of(Z_BASE + at * Z_SUB, 128), Z_SUB)
+
+    def x_copy(kind, d, to):
+        cols = (y_cols(yc), z_cols(zc), pl.ds(X_BASE, 4096 - X_BASE))[kind]
+        at = s if to else lax.rem(s + NX - d, NX)
+        dst = xg.at[at, :, cols]
+        return remote(
+            hs.at[0, :, cols] if to else dst, dst, xs_s.at[kind, d - 1], xs_r.at[kind, d - 1], device(0, 0, d)
+        )
+
+    def x_start(kind):
+        each(3, lambda i: x_copy(kind, i + 1, True).start())
+
     def info_copy(d, to):
         at = s if to else lax.rem(s + NX - d, NX)
         return remote(info.at[at], info.at[at], in_s.at[d - 1], in_r.at[d - 1], device(0, 0, d))
 
+    x_start(1)
+    x_start(0)
     each(3, lambda i: info_copy(i + 1, True).start())
 
-    def y_copy(dy, d, to):
+    half_w = pl.ds(0, 2048)
+
+    def w_copy():
+        return remote(w_hbm.at[0, half_w, :], w1h, pr_s.at[0], pr_r.at[0], partner)
+
+    load_w1 = pltpu.make_async_copy(w_hbm.at[0, pl.ds(2048, 2048), :], w1h, loc.at[4])
+
+    @pl.when(g == 1)
+    def _():
+        w_copy().start()
+        load_w1.start()
+
+    def y_copy(k, d, to):
         shard = lax.rem(s + NX - d, NX)
-        y = yc if to else lax.rem(yc + NY - dy, NY)
-        ref = xg.at[shard, :, y_cols(y)]
-        return remote(ref, ref, ys_s.at[dy - 1, d - 1], ys_r.at[dy - 1, d - 1], device(0, dy, 0))
+        dy = 1 + 2 * k
+        ref = xg.at[shard, :, y_cols(yc if to else lax.rem(yc + NY - dy, NY))]
+        return remote(ref, ref, ys_s.at[k, d - 1], ys_r.at[k, d - 1], device(0, dy, 0))
+
+    def y_relay(k, d, to):
+        shard = lax.rem(s + NX - d, NX)
+        dy = 1 + 2 * k
+        ref = xg.at[shard, :, y_half(lax.rem(yc + (NY - dy if to else 2), NY), k)]
+        return remote(ref, ref, ys_s.at[2 + k, d - 1], ys_r.at[2 + k, d - 1], device(0, dy, 0))
 
     def z_copy(dz, d, to):
         shard = lax.rem(s + NX - d, NX)
-        at = zc if to else lax.rem(zc + NZ - dz, NZ)
-        ref = xg.at[shard, z_rows(lax.rem(at, 2)), z_cols(lax.div(at, 2))]
+        ref = xg.at[shard, :, z_cols(zc if to else lax.rem(zc + NZ - dz, NZ))]
         return remote(ref, ref, zs_s.at[dz - 1, d - 1], zs_r.at[dz - 1, d - 1], device(dz, 0, 0))
-
-    def forward_y(i):
-        x_copy(0, i + 1, False).wait_recv()
-        each(3, lambda j: y_copy(j + 1, i + 1, True).start())
 
     def forward_z(i):
         x_copy(1, i + 1, False).wait_recv()
         each(7, lambda j: z_copy(j + 1, i + 1, True).start())
 
+    def forward_y(i):
+        x_copy(0, i + 1, False).wait_recv()
+        y_copy(0, i + 1, True).start()
+        y_copy(1, i + 1, True).start()
+
+    each(3, forward_z)
     each(3, forward_y)
-    each(3, forward_z)
+    x_start(2)
 
     each(3, lambda i: info_copy(i + 1, False).wait_recv())
     tall = jnp.transpose(jnp.concatenate([info[i] for i in range(4)] + [jnp.zeros((96, 128), F32)], axis=0))
@@ -179,23 +178,37 @@
         else:
             z[...] += product
 
-    accumulate(yc * SUB, SUB, first=True)
-
-    def take_y(i):
-        each(3, lambda j: y_copy(i + 1, j + 1, False).wait_recv())
-        accumulate(lax.rem(yc + NY - (i + 1), NY) * SUB, SUB)
-
-    each(3, take_y)
+    accumulate(yc * Y_SUB, Y_SUB, first=True)
+
+    def pass_y(i):
+        for k in range(2):
+            y_copy(k, i + 1, False).wait_recv()
+            y_relay(k, i + 1, True).start()
+
+    each(3, pass_y)
+
+    def add_y(i):
+        accumulate(lax.rem(yc + 1 + 2 * i, NY) * Y_SUB, Y_SUB)
+
+    each(2, add_y)
 
     each(3, lambda i: x_copy(2, i + 1, False).wait_recv())
     accumulate(X_BASE, 512)
     accumulate(X_BASE + 512, 512)
 
-    def take_z(dz):
-        each(3, lambda j: z_copy(dz, j + 1, False).wait_recv())
-
-    each(7, lambda j: take_z(j + 1))
-    each(4, lambda i: accumulate(Z_BASE + i * SUB, SUB))
+    def take_y(i):
+        y_relay(0, i + 1, False).wait_recv()
+        y_relay(1, i + 1, False).wait_recv()
+
+    each(3, take_y)
+    accumulate(lax.rem(yc + 2, NY) * Y_SUB, Y_SUB)
+
+    def take_z(i):
+        each(3, lambda j: z_copy(i + 1, j + 1, False).wait_recv())
+
+    each(7, take_z)
+    accumulate(Z_BASE, 512)
+    accumulate(Z_BASE + 512, 512)
 
     own = pl.ds(pl.multiple_of(g * 256, 256), 256)
     theirs = pl.ds(pl.multiple_of(other * 256, 256), 256)
@@ -215,6 +228,8 @@
     own_block = pltpu.make_async_copy(xg.at[:, :, block_cols(block)], xblk, loc.at[5])
     own_info = pltpu.make_async_copy(info, info1, loc.at[6])
     own_n1 = pltpu.make_async_copy(nrm.at[:, pl.ds(2048, 2048)], n1h, loc.at[7])
+
+    z_trade.wait()
 
     @pl.when(g == 1)
     def _():
@@ -224,8 +239,6 @@
         own_block.start()
         own_info.start()
         own_n1.start()
-
-    z_trade.wait_recv()
 
     lane = lax.broadcasted_iota(jnp.int32, (ROWS, 128), 1)
     column = lax.broadcasted_iota(jnp.int32, (ROWS, 896), 1)
@@ -309,11 +322,6 @@
     each(256 // ROWS, gradient)
     lg_trade = remote(lg.at[own, :], lg.at[own, :], pr_s.at[5], pr_r.at[5], partner)
     lg_trade.start()
-    along_row = jnp.transpose(statc[...])[0:8]
-    sub8w = lax.broadcasted_iota(jnp.int32, (8, 256), 0)
-    lossrt[g] = jnp.where(sub8w == 0, jnp.broadcast_to(loss, (8, 256)), along_row)
-    rt_trade = remote(lossrt.at[g], lossrt.at[g], pr_s.at[6], pr_r.at[6], partner)
-    rt_trade.start()
 
     @pl.when(g == 0)
     def _():
@@ -345,21 +353,27 @@
     def second(h):
         return yc + (s - yc) * h
 
-    def a_copy(h, d):
+    def a_copy(h, k, part):
+        d = 1 + 2 * k
         to = device(0, d * h, d * (1 - h))
-        return remote(ng.at[h, lax.rem(first(h) + d, 4)], r1.at[h, d - 1], ab_s.at[h, 0, d - 1], ab_r.at[h, 0, d - 1], to)
+        blocks = pl.ds(2 * ((k + part) % 2), 2)
+        sems = (ab_s.at[h, k, part], ab_r.at[h, k, part])
+        if part == 0:
+            return remote(ng.at[h, lax.rem(first(h) + 2, 4), blocks], q1.at[h, k], *sems, to)
+        src = ng.at[h, lax.rem(first(h) + d, 4), blocks] if part == 1 else q2.at[h, k]
+        return remote(src, r1.at[h, k, blocks], *sems, to)
 
     def at_copy(h, d):
         to = device(0, d * h, d * (1 - h))
-        return remote(lossrt.at[h], rt_r1.at[h, d - 1], ab_s.at[h, 1, d - 1], ab_r.at[h, 1, d - 1], to)
+        return remote(lossrt.at[h], rt_r1.at[h, d - 1], ab_s.at[h, 2, d - 1], ab_r.at[h, 2, d - 1], to)
 
     def b_copy(h, d):
         to = device(0, d * (1 - h), d * h)
-        return remote(s2.at[h, lax.rem(second(h) + d, 4)], r2.at[h, d - 1], ab_s.at[h, 2, d - 1], ab_r.at[h, 2, d - 1], to)
+        return remote(s2.at[h, lax.rem(second(h) + d, 4)], r2.at[h, d - 1], ab_s.at[h, 3, d - 1], ab_r.at[h, 3, d - 1], to)
 
     def bt_copy(h, d):
         to = device(0, d * (1 - h), d * h)
-        return remote(rt_s.at[h, 0], rt_r2.at[h, d - 1], ab_s.at[h, 3, d - 1], ab_r.at[h, 3, d - 1], to)
+        return remote(rt_s.at[h, 0], rt_r2.at[h, d - 1], ab_s.at[h, 4, d - 1], ab_r.at[h, 4, d - 1], to)
 
     def c_copy(h, d):
         return remote(s3.at[h, lax.rem(zc + d, NZ)], r3.at[h, d - 1], cz_s.at[h, 0, d - 1], cz_r.at[h, 0, d - 1], device(d, 0, 0))
@@ -368,24 +382,36 @@
         return remote(rt_s.at[h, 1], rt_r3.at[h, d - 1], cz_s.at[h, 1, d - 1], cz_r.at[h, 1, d - 1], device(d, 0, 0))
 
     def start_a(h):
-        def go(i):
-            a_copy(h, i + 1).start()
-            at_copy(h, i + 1).start()
-
-        each(3, go)
+        for part in range(2):
+            for k in range(2):
+                a_copy(h, k, part).start()
+
+    def start_at(h):
+        each(3, lambda i: at_copy(h, i + 1).start())
+
+    def pass_a(h):
+        for k in range(2):
+            a_copy(h, k, 0).wait_recv()
+            at = lax.rem(first(h) + 1 + 2 * k, 4)
+
+            def add(i, k=k, at=at):
+                for b in range(2):
+                    q2[h, k, b, i] = (ng[h, at, 2 * k + b, i].astype(F32) + q1[h, k, b, i].astype(F32)).astype(BF16)
+
+            each(NZ, add)
+            a_copy(h, k, 2).start()
 
     def start_b(h):
-        def got(i):
-            a_copy(h, i + 1).wait_recv()
-            at_copy(h, i + 1).wait_recv()
-
-        each(3, got)
+        each(3, lambda i: at_copy(h, i + 1).wait_recv())
+        for k in range(2):
+            a_copy(h, k, 1).wait_recv()
+            a_copy(h, k, 2).wait_recv()
         mine = first(h)
 
         def add(b):
             for k in range(NZ):
                 total = ng[h, mine, b, k].astype(F32)
-                for i in range(3):
+                for i in range(2):
                     total += r1[h, i, b, k].astype(F32)
                 s2[h, b, k] = total.astype(BF16)
 
@@ -434,10 +460,20 @@
 
     states_grad(g)
     start_a(g)
-    lg_trade.wait()
-    rt_trade.wait()
+    lg_trade.wait_recv()
     states_grad(other)
     start_a(other)
+
+    along_row = jnp.transpose(statc[...])[0:8]
+    sub8w = lax.broadcasted_iota(jnp.int32, (8, 256), 0)
+    lossrt[g] = jnp.where(sub8w == 0, jnp.broadcast_to(loss, (8, 256)), along_row)
+    rt_trade = remote(lossrt.at[g], lossrt.at[g], pr_s.at[6], pr_r.at[6], partner)
+    rt_trade.start()
+
+    start_at(g)
+    rt_trade.wait()
+    lg_trade.wait_send()
+    start_at(other)
 
     @pl.when(g == 0)
     def _():
@@ -457,16 +493,15 @@
 
     each(16, flip)
 
-    def head_store(i):
-        rows = pl.ds(pl.multiple_of(i * 512, 512), 512)
-        return pltpu.make_async_copy(hg.at[rows, :], head_out.at[rows, :], hg_s.at[i])
+    pass_a(g)
 
     def head_tile(i):
         rows = pl.ds(pl.multiple_of(i * 512, 512), 512)
-        hg[rows, :] = jnp.dot(n1t[rows, :], lg[...], preferred_element_type=F32).astype(BF16)
-        head_store(i).start()
-
-    each(4, head_tile)
+        head_out[rows, :] = jnp.dot(n1t[rows, :], lg[...], preferred_element_type=F32).astype(BF16)
+
+    each(2, head_tile)
+    pass_a(other)
+    each(2, lambda i: head_tile(i + 2))
 
     inv_row = jnp.concatenate([info1[i, 0:1] for i in range(4)], axis=1)
     for i in range(4):
@@ -494,7 +529,7 @@
         hidden_out[:, cols] = hidden.astype(BF16)
         gain_total += jnp.sum(grad * unit, axis=1, keepdims=True)
     wide = jnp.concatenate([jnp.broadcast_to(gain_total, (16, 128)), jnp.zeros((112, 128), F32)], axis=0)
-    gain_out[...] = jnp.transpose(wide)[0:1]
+    gain_out[...] = jnp.transpose(wide)[0:1, 0:16]
     loss_out[...] = lossrt[lax.div(s, 2), 0:1, pl.ds(pl.multiple_of(lax.rem(s, 2) * 128, 128), 128)]
 
     for kind in range(3):
@@ -502,11 +537,12 @@
 
     def sent_yz(i):
         info_copy(i + 1, True).wait_send()
-        each(3, lambda j: y_copy(j + 1, i + 1, True).wait_send())
+        for k in range(2):
+            y_copy(k, i + 1, True).wait_send()
+            y_relay(k, i + 1, True).wait_send()
         each(7, lambda j: z_copy(j + 1, i + 1, True).wait_send())
 
     each(3, sent_yz)
-    z_trade.wait_send()
 
     @pl.when(g == 1)
     def _():
@@ -520,7 +556,6 @@
 
     def sent_ab(h):
         def one(i):
-            a_copy(h, i + 1).wait_send()
             at_copy(h, i + 1).wait_send()
             b_copy(h, i + 1).wait_send()
             bt_copy(h, i + 1).wait_send()
@@ -529,11 +564,13 @@
             c_copy(h, i + 1).wait_send()
             ct_copy(h, i + 1).wait_send()
 
+        for part in range(3):
+            for k in range(2):
+                a_copy(h, k, part).wait_send()
         each(3, one)
         each(7, two)
 
     each(2, sent_ab)
-    each(4, lambda i: head_store(i).wait())
 
 
 def per_device(hidden_states, output_head_weights, norm_gains, label_ids):
@@ -566,7 +603,9 @@
         vm((2, 8, 256), F32),
         vm((256, 128), F32),
         vm((2, 4, 4, 8, 16, 256), BF16),
-        vm((2, 3, 4, 8, 16, 256), BF16),
+        vm((2, 2, 2, 8, 16, 256), BF16),
+        vm((2, 2, 2, 8, 16, 256), BF16),
+        vm((2, 2, 4, 8, 16, 256), BF16),
         vm((2, 4, 8, 16, 256), BF16),
         vm((2, 3, 8, 16, 256), BF16),
         vm((2, 8, 16, 256), BF16),
@@ -576,39 +615,37 @@
         vm((2, 3, 8, 256), F32),
         vm((2, 7, 8, 256), F32),
         vm((2, 16, 256), F32),
-        vm((2048, 896), BF16),
         dma((8,)),
         dma((3, 3)), dma((3, 3)),
-        dma((3, 3)), dma((3, 3)),
+        dma((4, 3)), dma((4, 3)),
         dma((7, 3)), dma((7, 3)),
         dma((3,)), dma((3,)),
         dma((7,)), dma((7,)),
         dma((2, 3)), dma((2, 3)),
         dma((7,)), dma((7,)),
-        dma((2, 4, 3)), dma((2, 4, 3)),
+        dma((2, 5, 3)), dma((2, 5, 3)),
         dma((2, 2, 7)), dma((2, 2, 7)),
-        dma((4,)),
     ]
-    whole = pl.BlockSpec(memory_space=pl.ANY)
+    whole = pl.BlockSpec(memory_space=pltpu.HBM)
     vmem = pl.BlockSpec(memory_space=pltpu.VMEM)
     loss, head_grad, hidden_grad, gain_grad = pl.pallas_call(
         kernel,
         name="distill",
         out_shape=(
-            jax.ShapeDtypeStruct((1, 128), F32),
-            jax.ShapeDtypeStruct((2048, 896), BF16),
-            jax.ShapeDtypeStruct((16, 512), BF16),
-            jax.ShapeDtypeStruct((1, 128), F32),
+            vm((1, 128), F32),
+            vm((2048, 896), BF16),
+            vm((16, 512), BF16),
+            vm((1, 16), F32),
         ),
         in_specs=[whole] * 4,
-        out_specs=(vmem, whole, vmem, vmem),
+        out_specs=(vmem,) * 4,
         scratch_shapes=scratch,
         cost_estimate=pl.CostEstimate(flops=10**10, bytes_accessed=2 * 10**7, transcendentals=10**6),
         compiler_params=pltpu.CompilerParams(
-            collective_id=0, has_side_effects=True, vmem_limit_bytes=60 * 2**20
+            collective_id=0, has_side_effects=True, vmem_limit_bytes=50 * 2**20
         ),
     )(hidden_states, output_head_weights, norm_gains, label_ids.reshape(1, 128))
-    return loss.reshape(128), head_grad, hidden_grad, gain_grad[0, :16]
+    return loss.reshape(128), head_grad, hidden_grad, gain_grad.reshape(16)
 
 
 def solution(mesh):

time: 104 us -> 87.2 us (0.84)
  Pallas kernels: 95.7 us -> 81.5 us
  local copies, waits for them, and re-layouts: 7.08 us -> 4.87 us
    pallas_call x1, Pallas kernels: 95.7 us -> 81.5 us  [per_device(): pl.pallas_call(kernel, name='distill', out_shape=(vm((1, 128), F32), vm((...]
    squeeze x1 -> x0, local copies, waits for them, and re-layouts: 1.18 us -> none  [per_device(): return (loss.reshape(128), head_grad, hidden_grad, gain_grad[0, :16])]
    unnamed x5 -> x8, local copies, waits for them, and re-layouts: 5.9 us -> 4.87 us
where the time goes in v2:
time: 87.2 us; the launch traced here: 87.1 us
  Pallas kernels  81.5 us (93%)
  local copies, waits for them, and re-layouts  4.87 us (6%)
    pallas_call x1, Pallas kernels, per_device(): pl.pallas_call(kernel, name='distill', out_shape=(vm((1, 128), F32), vm((...  81.5 us
    unnamed x8, local copies, waits for them, and re-layouts  4.87 us

profile of v2, /device:TPU:2, one launch (start us, length us, event | category | flops | bytes accessed | tf_op | source)
XLA Modules:
  0.0 87.1 jit_solution(8219708540644856743)
XLA Ops:
  0.6 0.0 copy-start
  0.6 0.7 copy-done
  1.4 0.0 copy-start.1
  1.4 0.7 copy-done.1
  2.0 81.5 %distill.1 = (f32[1,128]{1,0:T(1,128)S(1)}, bf16[2048,896]{1,0:T(8,128)(2,1)S(1)}, bf16[16,512]{1,0:T(8,128)(2,1)S(1)}, f32[1,16]{1,0:T(1,128)S(1)}) custom-call(bf16[1,128,4096]{2,1,0:T(8,128)(2,1)} %hs.1, bf16[1,4096,896]{2,1,0:T(8,128)(2,1)} %w_hbm.1, f32[2,4096]{1,0:T(2,128)S(1)} %copy-done, s32[1,128]{1,0:T(1,128)S(1)} %bitcast.5), custom_call_target="tpu_custom_call" | custom-call | flops 10000000000 | bytes 20000000 | tf_op jit(solution)/shard_map/distill/pallas_call | solution.py:631
  83.6 0.5 copy.12
  84.1 0.5 copy.15
  84.6 0.6 copy.14
  85.2 1.8 %copy.13 = bf16[2048,896]{1,0:T(8,128)(2,1)} copy(bf16[2048,896]{1,0:T(8,128)(2,1)S(1)} %get-tuple-element.13) | data formatting | bytes 7340032
Async XLA Ops:
  0.6 0.8 copy-start
  1.4 0.7 copy-start.1

commit v3 on v2

--- a/solution.py
+++ b/solution.py
@@ -65,12 +65,55 @@
     load_x.start()
     load_g.start()
     load_l.start()
-    load_w.start()
 
     barrier = pltpu.get_barrier_semaphore()
     for dz, dy, dx in PEERS:
         pl.semaphore_signal(barrier, inc=1, device_id=device(dz, dy, dx), device_id_type=MESH)
     pl.semaphore_signal(barrier, inc=1, device_id=partner, device_id_type=MESH)
+    pl.semaphore_wait(barrier, len(PEERS) + 1)
+
+    def y_cols(y, part):
+        return pl.ds(pl.multiple_of(y * Y_SUB + part * 256, 256), 256)
+
+    def y_half(y, part, k):
+        return pl.ds(pl.multiple_of(y * Y_SUB + part * 256 + k * 128, 128), 128)
+
+    def z_cols(at):
+        return pl.ds(pl.multiple_of(Z_BASE + at * Z_SUB, 128), Z_SUB)
+
+    def x_copy(kind, d, to):
+        cols = (z_cols(zc), y_cols(yc, 0), y_cols(yc, 1), pl.ds(X_BASE, 1024))[kind]
+        at = s if to else lax.rem(s + NX - d, NX)
+        dst = xg.at[at, :, cols]
+        return remote(
+            hs.at[0, :, cols] if to else dst, dst, xs_s.at[kind, d - 1], xs_r.at[kind, d - 1], device(0, 0, d)
+        )
+
+    def x_relay(k, to):
+        d = 1 + 2 * k
+        ref = xg.at[lax.rem(s + (NX - d if to else 2), NX), :, pl.ds(X_BASE + 512 * k, 512)]
+        return remote(ref, ref, xs_s.at[4, k], xs_r.at[4, k], device(0, 0, d))
+
+    def info_copy(d, to):
+        at = s if to else lax.rem(s + NX - d, NX)
+        return remote(info.at[at], info.at[at], in_s.at[d - 1], in_r.at[d - 1], device(0, 0, d))
+
+    for kind in range(3):
+        each(3, lambda i, kind=kind: x_copy(kind, i + 1, True).start())
+    load_w.start()
+
+    half_w = pl.ds(0, 2048)
+
+    def w_copy():
+        return remote(w_hbm.at[0, half_w, :], w1h, pr_s.at[0], pr_r.at[0], partner)
+
+    load_w1 = pltpu.make_async_copy(w_hbm.at[0, pl.ds(2048, 2048), :], w1h, loc.at[4])
+
+    @pl.when(g == 1)
+    def _():
+        w_copy().start()
+        load_w1.start()
+
     load_x.wait()
     load_g.wait()
     load_l.wait()
@@ -85,77 +128,60 @@
     label_rows = jnp.broadcast_to(label[...].astype(F32), (8, 128))
     info[s] = jnp.where(sub8 == 1, label_rows, inverse_rows)
 
-    pl.semaphore_wait(barrier, len(PEERS) + 1)
-
-    def y_cols(y):
-        return pl.ds(pl.multiple_of(y * Y_SUB, 128), Y_SUB)
-
-    def y_half(y, k):
-        return pl.ds(pl.multiple_of(y * Y_SUB + k * (Y_SUB // 2), 128), Y_SUB // 2)
-
-    def z_cols(at):
-        return pl.ds(pl.multiple_of(Z_BASE + at * Z_SUB, 128), Z_SUB)
-
-    def x_copy(kind, d, to):
-        cols = (y_cols(yc), z_cols(zc), pl.ds(X_BASE, 4096 - X_BASE))[kind]
-        at = s if to else lax.rem(s + NX - d, NX)
-        dst = xg.at[at, :, cols]
-        return remote(
-            hs.at[0, :, cols] if to else dst, dst, xs_s.at[kind, d - 1], xs_r.at[kind, d - 1], device(0, 0, d)
-        )
-
-    def x_start(kind):
-        each(3, lambda i: x_copy(kind, i + 1, True).start())
-
-    def info_copy(d, to):
-        at = s if to else lax.rem(s + NX - d, NX)
-        return remote(info.at[at], info.at[at], in_s.at[d - 1], in_r.at[d - 1], device(0, 0, d))
-
-    x_start(1)
-    x_start(0)
     each(3, lambda i: info_copy(i + 1, True).start())
 
-    half_w = pl.ds(0, 2048)
-
-    def w_copy():
-        return remote(w_hbm.at[0, half_w, :], w1h, pr_s.at[0], pr_r.at[0], partner)
-
-    load_w1 = pltpu.make_async_copy(w_hbm.at[0, pl.ds(2048, 2048), :], w1h, loc.at[4])
-
-    @pl.when(g == 1)
-    def _():
-        w_copy().start()
-        load_w1.start()
-
-    def y_copy(k, d, to):
+    def y_copy(part, k, d, to):
         shard = lax.rem(s + NX - d, NX)
         dy = 1 + 2 * k
-        ref = xg.at[shard, :, y_cols(yc if to else lax.rem(yc + NY - dy, NY))]
-        return remote(ref, ref, ys_s.at[k, d - 1], ys_r.at[k, d - 1], device(0, dy, 0))
-
-    def y_relay(k, d, to):
+        ref = xg.at[shard, :, y_cols(yc if to else lax.rem(yc + NY - dy, NY), part)]
+        return remote(ref, ref, ys_s.at[part, k, d - 1], ys_r.at[part, k, d - 1], device(0, dy, 0))
+
+    def y_relay(part, k, d, to):
         shard = lax.rem(s + NX - d, NX)
         dy = 1 + 2 * k
-        ref = xg.at[shard, :, y_half(lax.rem(yc + (NY - dy if to else 2), NY), k)]
-        return remote(ref, ref, ys_s.at[2 + k, d - 1], ys_r.at[2 + k, d - 1], device(0, dy, 0))
-
-    def z_copy(dz, d, to):
+        ref = xg.at[shard, :, y_half(lax.rem(yc + (NY - dy if to else 2), NY), part, k)]
+        return remote(ref, ref, ys_s.at[part, 2 + k, d - 1], ys_r.at[part, 2 + k, d - 1], device(0, dy, 0))
+
+    def z_copy(slot, d, to):
         shard = lax.rem(s + NX - d, NX)
-        ref = xg.at[shard, :, z_cols(zc if to else lax.rem(zc + NZ - dz, NZ))]
-        return remote(ref, ref, zs_s.at[dz - 1, d - 1], zs_r.at[dz - 1, d - 1], device(dz, 0, 0))
+        k = slot % 2
+        hops = (2, 1, 1, 2)[slot // 2]
+        far = (2, 1, 3, 4)[slot // 2]
+        step = NZ - hops if k else hops
+        away = far if k else NZ - far
+        at = lax.rem(zc + (away + step) % NZ, NZ) if to else lax.rem(zc + away, NZ)
+        rows = pl.ds(64 * k, 64) if slot >= 6 else pl.ds(0, 128)
+        ref = xg.at[shard, rows, z_cols(at)]
+        return remote(ref, ref, zs_s.at[slot, d - 1], zs_r.at[slot, d - 1], device(step, 0, 0))
 
     def forward_z(i):
-        x_copy(1, i + 1, False).wait_recv()
-        each(7, lambda j: z_copy(j + 1, i + 1, True).start())
-
-    def forward_y(i):
         x_copy(0, i + 1, False).wait_recv()
-        y_copy(0, i + 1, True).start()
-        y_copy(1, i + 1, True).start()
+        for slot in range(4):
+            z_copy(slot, i + 1, True).start()
+
+    def pass_z(i):
+        for k in range(2):
+            z_copy(k, i + 1, False).wait_recv()
+            z_copy(4 + k, i + 1, True).start()
+            z_copy(6 + k, i + 1, True).start()
+
+    def forward_y(part, i):
+        x_copy(1 + part, i + 1, False).wait_recv()
+        for k in range(2):
+            y_copy(part, k, i + 1, True).start()
+
+    def pass_y(part, i):
+        for k in range(2):
+            y_copy(part, k, i + 1, False).wait_recv()
+            y_relay(part, k, i + 1, True).start()
 
     each(3, forward_z)
-    each(3, forward_y)
-    x_start(2)
+    each(3, lambda i: forward_y(0, i))
+    each(3, lambda i: forward_y(1, i))
+    for k in range(2):
+        x_copy(3, 1 + 2 * k, True).start()
+    each(3, pass_z)
+    each(3, lambda i: pass_y(0, i))
 
     each(3, lambda i: info_copy(i + 1, False).wait_recv())
     tall = jnp.transpose(jnp.concatenate([info[i] for i in range(4)] + [jnp.zeros((96, 128), F32)], axis=0))
@@ -164,13 +190,16 @@
         labb[pl.ds(128 * i, 128), :] = jnp.broadcast_to(tall[:, 8 * i + 1 : 8 * i + 2], (128, 128))
     load_w.wait()
 
-    def accumulate(f0, width, first=False):
+    def normalized(f0, width):
         for b in range(width // 128):
             cols = pl.ds(pl.multiple_of(f0 + b * 128, 128), 128)
             gain = jnp.where(is_teacher, gains[0:1, cols], gains[1:2, cols])
             for i in range(4):
                 unit = xg[i, :, cols].astype(F32) * invb[i]
                 nrm[pl.ds(i * 128, 128), cols] = (unit * gain).astype(BF16)
+
+    def accumulate(f0, width, first=False):
+        normalized(f0, width)
         cols = pl.ds(pl.multiple_of(f0, 128), width)
         product = jnp.dot(nrm[:, cols], w[cols, :], preferred_element_type=F32)
         if first:
@@ -179,41 +208,49 @@
             z[...] += product
 
     accumulate(yc * Y_SUB, Y_SUB, first=True)
-
-    def pass_y(i):
-        for k in range(2):
-            y_copy(k, i + 1, False).wait_recv()
-            y_relay(k, i + 1, True).start()
-
-    each(3, pass_y)
+    each(3, lambda i: pass_y(1, i))
+    for k in range(2):
+        x_copy(3, 1 + 2 * k, False).wait_recv()
+        x_relay(k, True).start()
 
     def add_y(i):
         accumulate(lax.rem(yc + 1 + 2 * i, NY) * Y_SUB, Y_SUB)
 
     each(2, add_y)
 
-    each(3, lambda i: x_copy(2, i + 1, False).wait_recv())
-    accumulate(X_BASE, 512)
-    accumulate(X_BASE + 512, 512)
+    def take_z(i):
+        for slot in range(2, 8):
+            z_copy(slot, i + 1, False).wait_recv()
+
+    each(3, take_z)
+    accumulate(Z_BASE, 512)
+    accumulate(Z_BASE + 512, 512)
 
     def take_y(i):
-        y_relay(0, i + 1, False).wait_recv()
-        y_relay(1, i + 1, False).wait_recv()
+        for part in range(2):
+            for k in range(2):
+                y_relay(part, k, i + 1, False).wait_recv()
 
     each(3, take_y)
     accumulate(lax.rem(yc + 2, NY) * Y_SUB, Y_SUB)
-
-    def take_z(i):
-        each(3, lambda j: z_copy(i + 1, j + 1, False).wait_recv())
-
-    each(7, take_z)
-    accumulate(Z_BASE, 512)
-    accumulate(Z_BASE + 512, 512)
+    x_relay(0, False).wait_recv()
+    accumulate(X_BASE, 512)
+    x_relay(1, False).wait_recv()
 
     own = pl.ds(pl.multiple_of(g * 256, 256), 256)
     theirs = pl.ds(pl.multiple_of(other * 256, 256), 256)
-    z_trade = remote(z.at[theirs, :], zp, pr_s.at[1], pr_r.at[1], partner)
-    z_trade.start()
+    halves = ((0, 512), (512, 384))
+
+    def z_trade(k):
+        cols = pl.ds(*halves[k])
+        return remote(z.at[theirs, cols], zp.at[:, cols], pr_s.at[(1, 7)[k]], pr_r.at[(1, 7)[k]], partner)
+
+    normalized(X_BASE + 512, 512)
+    for k in range(2):
+        last = pl.ds(X_BASE + 512, 512)
+        cols = pl.ds(*halves[k])
+        z[:, cols] += jnp.dot(nrm[:, last], w[last, cols], preferred_element_type=F32)
+        z_trade(k).start()
 
     vs = v * NX + s
     teacher_block = lax.div(vs, 8)
@@ -229,7 +266,8 @@
     own_info = pltpu.make_async_copy(info, info1, loc.at[6])
     own_n1 = pltpu.make_async_copy(nrm.at[:, pl.ds(2048, 2048)], n1h, loc.at[7])
 
-    z_trade.wait()
+    for k in range(2):
+        z_trade(k).wait()
 
     @pl.when(g == 1)
     def _():
@@ -534,13 +572,18 @@
 
     for kind in range(3):
         each(3, lambda i, kind=kind: x_copy(kind, i + 1, True).wait_send())
+    for k in range(2):
+        x_copy(3, 1 + 2 * k, True).wait_send()
+        x_relay(k, True).wait_send()
 
     def sent_yz(i):
         info_copy(i + 1, True).wait_send()
-        for k in range(2):
-            y_copy(k, i + 1, True).wait_send()
-            y_relay(k, i + 1, True).wait_send()
-        each(7, lambda j: z_copy(j + 1, i + 1, True).wait_send())
+        for part in range(2):
+            for k in range(2):
+                y_copy(part, k, i + 1, True).wait_send()
+                y_relay(part, k, i + 1, True).wait_send()
+        for slot in range(8):
+            z_copy(slot, i + 1, True).wait_send()
 
     each(3, sent_yz)
 
@@ -571,6 +614,15 @@
         each(7, two)
 
     each(2, sent_ab)
+
+
+def store(loss, head, hidden, gain, loss_out, head_out, hidden_out, gain_out, sems):
+    pairs = ((head, head_out), (hidden, hidden_out), (loss, loss_out), (gain, gain_out))
+    copies = [pltpu.make_async_copy(a, b, sems.at[i]) for i, (a, b) in enumerate(pairs)]
+    for copy in copies:
+        copy.start()
+    for copy in copies:
+        copy.wait()
 
 
 def per_device(hidden_states, output_head_weights, norm_gains, label_ids):
@@ -616,11 +668,11 @@
         vm((2, 7, 8, 256), F32),
         vm((2, 16, 256), F32),
         dma((8,)),
-        dma((3, 3)), dma((3, 3)),
-        dma((4, 3)), dma((4, 3)),
-        dma((7, 3)), dma((7, 3)),
+        dma((5, 3)), dma((5, 3)),
+        dma((2, 4, 3)), dma((2, 4, 3)),
+        dma((8, 3)), dma((8, 3)),
         dma((3,)), dma((3,)),
-        dma((7,)), dma((7,)),
+        dma((8,)), dma((8,)),
         dma((2, 3)), dma((2, 3)),
         dma((7,)), dma((7,)),
         dma((2, 5, 3)), dma((2, 5, 3)),
@@ -642,9 +694,17 @@
         scratch_shapes=scratch,
         cost_estimate=pl.CostEstimate(flops=10**10, bytes_accessed=2 * 10**7, transcendentals=10**6),
         compiler_params=pltpu.CompilerParams(
-            collective_id=0, has_side_effects=True, vmem_limit_bytes=50 * 2**20
+            collective_id=0, has_side_effects=True, vmem_limit_bytes=59 * 2**20
         ),
     )(hidden_states, output_head_weights, norm_gains, label_ids.reshape(1, 128))
+    loss, head_grad, hidden_grad, gain_grad = pl.pallas_call(
+        store,
+        name="store",
+        out_shape=[jax.ShapeDtypeStruct(a.shape, a.dtype) for a in (loss, head_grad, hidden_grad, gain_grad)],
+        in_specs=[vmem] * 4,
+        out_specs=[pl.BlockSpec(memory_space=pltpu.HBM)] * 4,
+        scratch_shapes=[dma((4,))],
+    )(loss, head_grad, hidden_grad, gain_grad)
     return loss.reshape(128), head_grad, hidden_grad, gain_grad.reshape(16)
 
 

time: 87.2 us -> 88.8 us (1.018)
  Pallas kernels: 81.5 us -> 83.7 us
  local copies, waits for them, and re-layouts: 4.87 us -> 3.46 us
    pallas_call x0 -> x1, Pallas kernels: none -> 3.92 us  [per_device(): pl.pallas_call(store, name='store', out_shape=[jax.ShapeDtypeStruct(a.sha...]
    pallas_call x1, Pallas kernels: 81.5 us -> 79.8 us  [per_device(): pl.pallas_call(kernel, name='distill', out_shape=(vm((1, 128), F32), vm((...]
    unnamed x8, local copies, waits for them, and re-layouts: 4.87 us -> 3.46 us
where the time goes in v3:
time: 88.8 us; the launch traced here: 87.9 us
  Pallas kernels  83.7 us (94%)
  local copies, waits for them, and re-layouts  3.46 us (4%)
    pallas_call x1, Pallas kernels, per_device(): pl.pallas_call(kernel, name='distill', out_shape=(vm((1, 128), F32), vm((...  79.8 us
    pallas_call x1, Pallas kernels, per_device(): pl.pallas_call(store, name='store', out_shape=[jax.ShapeDtypeStruct(a.sha...  3.92 us
    unnamed x8, local copies, waits for them, and re-layouts  3.46 us

profile of v3, /device:TPU:2, one launch (start us, length us, event | category | flops | bytes accessed | tf_op | source)
XLA Modules:
  0.0 87.9 jit_solution(3035980818322674157)
XLA Ops:
  0.6 79.8 %distill.1 = (f32[1,128]{1,0:T(1,128)S(1)}, bf16[2048,896]{1,0:T(8,128)(2,1)S(1)}, bf16[16,512]{1,0:T(8,128)(2,1)S(1)}, f32[1,16]{1,0:T(1,128)S(1)}) custom-call(bf16[1,128,4096]{2,1,0:T(8,128)(2,1)} %hs.1, bf16[1,4096,896]{2,1,0:T(8,128)(2,1)} %w_hbm.1, f32[2,4096]{1,0:T(2,128)} %gains_hbm.1, s32[1,128]{1,0:T(1,128)} %bitcast.3), custom_call_target="tpu_custom_call" | custom-call | flops 10000000000 | bytes 20000000 | tf_op jit(solution)/shard_map/distill/pallas_call | solution.py:683
  80.5 0.0 copy-start
  80.5 1.8 %copy-done = bf16[2048,896]{1,0:T(8,128)(2,1)} copy-done((bf16[2048,896]{1,0:T(8,128)(2,1)}, bf16[2048,896]{1,0:T(8,128)(2,1)S(1)}, u32[]{:S(2)}) %copy-start) | copy-done | bytes 3670040
  82.3 0.0 copy-start.1
  82.3 0.6 copy-done.1
  82.9 0.0 copy-start.2
  82.9 0.5 copy-done.2
  83.4 0.0 copy-start.3
  83.4 0.6 copy-done.3
  83.9 3.9 %store.1 = (f32[1,128]{1,0:T(1,128)}, bf16[2048,896]{1,0:T(8,128)(2,1)}, bf16[16,512]{1,0:T(8,128)(2,1)}, f32[1,16]{1,0:T(1,128)}) custom-call(f32[1,128]{1,0:T(1,128)} %copy-done.2, bf16[2048,896]{1,0:T(8,128)(2,1)} %copy-done, bf16[16,512]{1,0:T(8,128)(2,1)} %copy-done.1, f32[1,16]{1,0:T(1,128)} %copy-done.3), custom_call_target="tpu_custom_call" | custom-call | tf_op jit(solution)/shard_map/store/pallas_call | solution.py:700
Async XLA Ops:
  80.5 1.8 %copy-start = (bf16[2048,896]{1,0:T(8,128)(2,1)}, bf16[2048,896]{1,0:T(8,128)(2,1)S(1)}, u32[]{:S(2)}) copy-start(bf16[2048,896]{1,0:T(8,128)(2,1)S(1)} %get-tuple-element.13.head) | copy-start | bytes 11010052
  82.3 0.6 copy-start.1
  82.9 0.5 copy-start.2
  83.4 0.6 copy-start.3

commit v4 on v3

--- a/solution.py
+++ b/solution.py
@@ -29,9 +29,9 @@
 def kernel(
     hs, w_hbm, gains_hbm, label_hbm,
     loss_out, head_out, hidden_out, gain_out,
-    xg, nrm, w, w1h, n1h, n1t, z, zp, e0s, e1s, z1s, lg,
+    xg, nrm, w, w1h, n1h, n1t, z, zp, e_own, e_given, lg,
     info, info1, invb, labb, gains, label, xblk, ut,
-    statc, st_send, st_recv, lossrt, colb,
+    statc, st_send, st_recv, losses, colb, gainb,
     ng, q1, q2, r1, s2, r2, s3, r3, rt_s, rt_r1, rt_r2, rt_r3, fin,
     loc, xs_s, xs_r, ys_s, ys_r, zs_s, zs_r, in_s, in_r, pr_s, pr_r,
     sa_s, sa_r, sz_s, sz_r, ab_s, ab_r, cz_s, cz_r,
@@ -98,8 +98,11 @@
         at = s if to else lax.rem(s + NX - d, NX)
         return remote(info.at[at], info.at[at], in_s.at[d - 1], in_r.at[d - 1], device(0, 0, d))
 
-    for kind in range(3):
-        each(3, lambda i, kind=kind: x_copy(kind, i + 1, True).start())
+    def x_start(kind):
+        each(3, lambda i: x_copy(kind, i + 1, True).start())
+
+    x_start(0)
+    x_start(1)
     load_w.start()
 
     half_w = pl.ds(0, 2048)
@@ -176,10 +179,11 @@
             y_relay(part, k, i + 1, True).start()
 
     each(3, forward_z)
+    x_start(2)
     each(3, lambda i: forward_y(0, i))
-    each(3, lambda i: forward_y(1, i))
     for k in range(2):
         x_copy(3, 1 + 2 * k, True).start()
+    each(3, lambda i: forward_y(1, i))
     each(3, pass_z)
     each(3, lambda i: pass_y(0, i))
 
@@ -252,7 +256,29 @@
         z[:, cols] += jnp.dot(nrm[:, last], w[last, cols], preferred_element_type=F32)
         z_trade(k).start()
 
+    lane = lax.broadcasted_iota(jnp.int32, (ROWS, 128), 1)
+    column = lax.broadcasted_iota(jnp.int32, (ROWS, 896), 1)
     vs = v * NX + s
+
+    def half_rows(r):
+        return pl.ds(pl.multiple_of(r * ROWS, ROWS), ROWS)
+
+    def own_rows(r):
+        return pl.ds(pl.multiple_of(g * 256 + r * ROWS, ROWS), ROWS)
+
+    def labels_at(r):
+        return labb[own_rows(r), 0:1].astype(jnp.int32) - vs * 896
+
+    def own_totals(r):
+        rows = half_rows(r)
+        mine = z[own_rows(r), :] * (1.0 / SOFTEN_TEMP)
+        top = jnp.max(mine, axis=1, keepdims=True)
+        e = jnp.exp(mine - top)
+        e_own[rows, :] = e
+        total = jnp.sum(e, axis=1, keepdims=True)
+        statc[rows, :] = jnp.where(lane == 0, top, jnp.broadcast_to(total, (ROWS, 128)))
+
+    each(256 // ROWS, own_totals)
     teacher_block = lax.div(vs, 8)
     block = g * 16 + teacher_block
 
@@ -268,6 +294,7 @@
 
     for k in range(2):
         z_trade(k).wait()
+
 
     @pl.when(g == 1)
     def _():
@@ -278,34 +305,28 @@
         own_info.start()
         own_n1.start()
 
-    lane = lax.broadcasted_iota(jnp.int32, (ROWS, 128), 1)
-    column = lax.broadcasted_iota(jnp.int32, (ROWS, 896), 1)
-
-    def labels_at(r):
-        rows = pl.ds(pl.multiple_of(g * 256 + r * ROWS, ROWS), ROWS)
-        return labb[rows, 0:1].astype(jnp.int32) - vs * 896
-
     def totals(r):
-        rows = pl.ds(pl.multiple_of(r * ROWS, ROWS), ROWS)
-        mine = z[pl.ds(pl.multiple_of(g * 256 + r * ROWS, ROWS), ROWS), :] * (1.0 / SOFTEN_TEMP)
+        rows = half_rows(r)
+        mine = z[own_rows(r), :] * (1.0 / SOFTEN_TEMP)
         given = zp[rows, :] * (1.0 / SOFTEN_TEMP)
-        z0 = jnp.where(is_teacher, mine, given)
+        top = jnp.max(given, axis=1, keepdims=True)
+        e = jnp.exp(given - top)
+        e_given[rows, :] = e
+        total = jnp.sum(e, axis=1, keepdims=True)
+        e0 = jnp.where(is_teacher, e_own[rows, :], e)
+        gap = jnp.where(is_teacher, mine - given, given - mine)
+        cross = jnp.sum(e0 * gap, axis=1, keepdims=True)
         z1 = jnp.where(is_teacher, given, mine)
-        m0 = jnp.max(z0, axis=1, keepdims=True)
-        m1 = jnp.max(z1, axis=1, keepdims=True)
-        e0 = jnp.exp(z0 - m0)
-        e1 = jnp.exp(z1 - m1)
-        e0s[rows, :] = e0
-        e1s[rows, :] = e1
-        z1s[rows, :] = z1
-        t0 = jnp.sum(e0, axis=1, keepdims=True)
-        t1 = jnp.sum(e1, axis=1, keepdims=True)
-        cross = jnp.sum(e0 * (z0 - z1), axis=1, keepdims=True)
         picked = jnp.sum(jnp.where(column == labels_at(r), z1, 0.0), axis=1, keepdims=True)
-        stats = jnp.zeros((ROWS, 128), F32)
-        for i, value in enumerate((m0, t0, cross, m1, t1, picked)):
-            stats = jnp.where(lane == i, value, stats)
-        statc[rows, :] = stats
+        stats = statc[rows, :]
+        own_at = jnp.where(is_teacher, 0, 3)
+        own_top, own_total = stats[:, 0:1], stats[:, 1:2]
+        for i, value in enumerate((own_top, own_total)):
+            stats = jnp.where(lane == own_at + i, value, stats)
+        for i, value in enumerate((top, total)):
+            stats = jnp.where(lane == 3 - own_at + i, value, stats)
+        stats = jnp.where(lane == 2, cross, stats)
+        statc[rows, :] = jnp.where(lane == 5, picked, stats)
 
     each(256 // ROWS, totals)
     local = jnp.transpose(statc[...])[0:8]
@@ -332,42 +353,70 @@
         sems = (sz_s.at[d - 1], sz_r.at[d - 1]) if axis == 2 else (sa_s.at[axis, d - 1], sa_r.at[axis, d - 1])
         return remote(st_send.at[axis], st_recv.at[axis * 3 + d - 1], *sems, to)
 
+    def prepare():
+        @pl.when(g == 0)
+        def _():
+            n1_copy.wait_recv()
+            xblk_copy.wait_recv()
+            info_pair.wait_recv()
+
+        @pl.when(g == 1)
+        def _():
+            own_n1.wait()
+            own_block.wait()
+            own_info.wait()
+
+        def flip(i):
+            cols = pl.ds(pl.multiple_of(i * 128, 128), 128)
+            n1t[cols, :] = jnp.transpose(n1h[:, cols])
+
+        each(16, flip)
+
+        for i in range(4):
+            unit = jnp.transpose(xblk[i].astype(F32)) * info1[i, 0:1]
+            ut[:, pl.ds(i * 128, 128)] = unit
+        gain_col = jnp.transpose(jnp.broadcast_to(gains[1:2, block_cols(block)], (128, 128)))
+        gainb[...] = gain_col
+
+        @pl.when(g == 0)
+        def _():
+            w_copy().wait_recv()
+
+        @pl.when(g == 1)
+        def _():
+            load_w1.wait()
+
     merged = local
     for axis, count in ((0, 3), (1, 3), (2, 7)):
         if axis:
             st_send[axis] = merged
         each(count, lambda i, axis=axis: st_copy(axis, i + 1).start())
+        if axis == 2:
+            prepare()
         each(count, lambda i, axis=axis: st_copy(axis, i + 1).wait_recv())
         merged = merge([merged] + [st_recv[axis * 3 + i] for i in range(count)])
 
     lse0 = merged[0:1] + jnp.log(merged[1:2])
     lse1 = merged[3:4] + jnp.log(merged[4:5])
     loss = merged[2:3] / merged[1:2] - lse0 + lse1 + LABEL_WEIGHT * (lse1 - merged[5:6])
+    losses[g] = loss
+    loss_trade = remote(losses.at[g], losses.at[g], pr_s.at[8], pr_r.at[8], partner)
     scale = 128 * 896 / 16.0 / SOFTEN_TEMP
-    a0 = scale * jnp.exp(local[0:1] - lse0)
+    a0 = -scale * jnp.exp(local[0:1] - lse0)
     a1 = (scale * (1.0 + LABEL_WEIGHT)) * jnp.exp(local[3:4] - lse1)
-    colb[...] = jnp.transpose(jnp.concatenate([a0, a1, jnp.zeros((126, 256), F32)], axis=0))
+    pair = [jnp.where(is_teacher, a0, a1), jnp.where(is_teacher, a1, a0)]
+    colb[...] = jnp.transpose(jnp.concatenate(pair + [jnp.zeros((126, 256), F32)], axis=0))
 
     def gradient(r):
-        rows = pl.ds(pl.multiple_of(r * ROWS, ROWS), ROWS)
+        rows = half_rows(r)
         cols = colb[rows, :]
         target = jnp.where(column == labels_at(r), scale * LABEL_WEIGHT, 0.0)
-        grad = (cols[:, 1:2] * e1s[rows, :] - cols[:, 0:1] * e0s[rows, :] - target).astype(BF16)
-        lg[pl.ds(pl.multiple_of(g * 256 + r * ROWS, ROWS), ROWS), :] = grad
-        along = jnp.sum(grad.astype(F32) * z1s[rows, :], axis=1, keepdims=True)
-        statc[rows, :] = jnp.broadcast_to(along, (ROWS, 128))
+        lg[own_rows(r), :] = (cols[:, 0:1] * e_own[rows, :] + cols[:, 1:2] * e_given[rows, :] - target).astype(BF16)
 
     each(256 // ROWS, gradient)
     lg_trade = remote(lg.at[own, :], lg.at[own, :], pr_s.at[5], pr_r.at[5], partner)
     lg_trade.start()
-
-    @pl.when(g == 0)
-    def _():
-        w_copy().wait_recv()
-
-    @pl.when(g == 1)
-    def _():
-        load_w1.wait()
+    loss_trade.start()
 
     def states_grad(h):
         tokens = lg[pl.ds(pl.multiple_of(h * 256, 256), 256), :]
@@ -403,7 +452,7 @@
 
     def at_copy(h, d):
         to = device(0, d * h, d * (1 - h))
-        return remote(lossrt.at[h], rt_r1.at[h, d - 1], ab_s.at[h, 2, d - 1], ab_r.at[h, 2, d - 1], to)
+        return remote(rt_s.at[h, 3], rt_r1.at[h, d - 1], ab_s.at[h, 2, d - 1], ab_r.at[h, 2, d - 1], to)
 
     def b_copy(h, d):
         to = device(0, d * (1 - h), d * h)
@@ -454,7 +503,7 @@
                 s2[h, b, k] = total.astype(BF16)
 
         each(4, add)
-        rt_s[h, 0] = lossrt[h] + rt_r1[h, 0] + rt_r1[h, 1] + rt_r1[h, 2]
+        rt_s[h, 0] = rt_s[h, 3] + rt_r1[h, 0] + rt_r1[h, 1] + rt_r1[h, 2]
 
         def go(i):
             b_copy(h, i + 1).start()
@@ -502,51 +551,32 @@
     states_grad(other)
     start_a(other)
 
-    along_row = jnp.transpose(statc[...])[0:8]
-    sub8w = lax.broadcasted_iota(jnp.int32, (8, 256), 0)
-    lossrt[g] = jnp.where(sub8w == 0, jnp.broadcast_to(loss, (8, 256)), along_row)
-    rt_trade = remote(lossrt.at[g], lossrt.at[g], pr_s.at[6], pr_r.at[6], partner)
+    def along(r):
+        rows = pl.ds(pl.multiple_of(r * ROWS, ROWS), ROWS)
+        grad = lg[pl.ds(pl.multiple_of(g * 256 + r * ROWS, ROWS), ROWS), :].astype(F32)
+        z1 = jnp.where(is_teacher, zp[rows, :], z[pl.ds(pl.multiple_of(g * 256 + r * ROWS, ROWS), ROWS), :])
+        total = jnp.sum(grad * z1, axis=1, keepdims=True) * (1.0 / SOFTEN_TEMP)
+        statc[rows, :] = jnp.broadcast_to(total, (ROWS, 128))
+
+    each(256 // ROWS, along)
+    rt_s[g, 3] = jnp.transpose(statc[...])[0:1]
+    rt_trade = remote(rt_s.at[g, 3], rt_s.at[g, 3], pr_s.at[6], pr_r.at[6], partner)
     rt_trade.start()
-
     start_at(g)
     rt_trade.wait()
     lg_trade.wait_send()
+    loss_trade.wait()
     start_at(other)
-
-    @pl.when(g == 0)
-    def _():
-        n1_copy.wait_recv()
-        xblk_copy.wait_recv()
-        info_pair.wait_recv()
-
-    @pl.when(g == 1)
-    def _():
-        own_n1.wait()
-        own_block.wait()
-        own_info.wait()
-
-    def flip(i):
-        cols = pl.ds(pl.multiple_of(i * 128, 128), 128)
-        n1t[cols, :] = jnp.transpose(n1h[:, cols])
-
-    each(16, flip)
-
-    pass_a(g)
 
     def head_tile(i):
         rows = pl.ds(pl.multiple_of(i * 512, 512), 512)
         head_out[rows, :] = jnp.dot(n1t[rows, :], lg[...], preferred_element_type=F32).astype(BF16)
 
     each(2, head_tile)
+    pass_a(g)
+    head_tile(2)
     pass_a(other)
-    each(2, lambda i: head_tile(i + 2))
-
-    inv_row = jnp.concatenate([info1[i, 0:1] for i in range(4)], axis=1)
-    for i in range(4):
-        unit = jnp.transpose(xblk[i].astype(F32)) * info1[i, 0:1]
-        ut[:, pl.ds(i * 128, 128)] = unit
-    gain_col = jnp.transpose(jnp.broadcast_to(gains[1:2, block_cols(block)], (128, 128)))
-    statc[pl.ds(0, 128), :] = gain_col
+    head_tile(3)
 
     start_b(g)
     start_b(other)
@@ -555,20 +585,21 @@
     finish(g)
     finish(other)
 
+    inv_row = jnp.concatenate([info1[i, 0:1] for i in range(4)], axis=1)
     mine16 = pl.ds(pl.multiple_of(lax.rem(vs, 8) * 16, 16), 16)
-    gain16 = statc[mine16, 0:1]
+    gain16 = gainb[mine16, 0:1]
     gain_total = jnp.zeros((16, 1), F32)
     for h in range(2):
         cols = pl.ds(h * 256, 256)
         unit = ut[mine16, cols]
         grad = fin[h]
-        row_mean = rt_s[h, 2][1:2] * (SOFTEN_TEMP / 4096)
+        row_mean = rt_s[h, 2] * (SOFTEN_TEMP / 4096)
         hidden = inv_row[:, h * 256 : h * 256 + 256] * (grad * gain16 - unit * row_mean)
         hidden_out[:, cols] = hidden.astype(BF16)
         gain_total += jnp.sum(grad * unit, axis=1, keepdims=True)
     wide = jnp.concatenate([jnp.broadcast_to(gain_total, (16, 128)), jnp.zeros((112, 128), F32)], axis=0)
     gain_out[...] = jnp.transpose(wide)[0:1, 0:16]
-    loss_out[...] = lossrt[lax.div(s, 2), 0:1, pl.ds(pl.multiple_of(lax.rem(s, 2) * 128, 128), 128)]
+    loss_out[...] = losses[lax.div(s, 2), :, pl.ds(pl.multiple_of(lax.rem(s, 2) * 128, 128), 128)]
 
     for kind in range(3):
         each(3, lambda i, kind=kind: x_copy(kind, i + 1, True).wait_send())
@@ -636,7 +667,6 @@
         vm((512, 2048), BF16),
         vm((2048, 512), BF16),
         vm((512, 896), F32),
-        vm((256, 896), F32),
         vm((256, 896), F32),
         vm((256, 896), F32),
         vm((256, 896), F32),
@@ -652,8 +682,9 @@
         vm((256, 128), F32),
         vm((3, 8, 256), F32),
         vm((13, 8, 256), F32),
-        vm((2, 8, 256), F32),
+        vm((2, 1, 256), F32),
         vm((256, 128), F32),
+        vm((128, 128), F32),
         vm((2, 4, 4, 8, 16, 256), BF16),
         vm((2, 2, 2, 8, 16, 256), BF16),
         vm((2, 2, 2, 8, 16, 256), BF16),
@@ -662,17 +693,17 @@
         vm((2, 3, 8, 16, 256), BF16),
         vm((2, 8, 16, 256), BF16),
         vm((2, 7, 16, 256), BF16),
-        vm((2, 3, 8, 256), F32),
-        vm((2, 3, 8, 256), F32),
-        vm((2, 3, 8, 256), F32),
-        vm((2, 7, 8, 256), F32),
+        vm((2, 4, 1, 256), F32),
+        vm((2, 3, 1, 256), F32),
+        vm((2, 3, 1, 256), F32),
+        vm((2, 7, 1, 256), F32),
         vm((2, 16, 256), F32),
         dma((8,)),
         dma((5, 3)), dma((5, 3)),
         dma((2, 4, 3)), dma((2, 4, 3)),
         dma((8, 3)), dma((8, 3)),
         dma((3,)), dma((3,)),
-        dma((8,)), dma((8,)),
+        dma((9,)), dma((9,)),
         dma((2, 3)), dma((2, 3)),
         dma((7,)), dma((7,)),
         dma((2, 5, 3)), dma((2, 5, 3)),
@@ -704,6 +735,7 @@
         in_specs=[vmem] * 4,
         out_specs=[pl.BlockSpec(memory_space=pltpu.HBM)] * 4,
         scratch_shapes=[dma((4,))],
+        compiler_params=pltpu.CompilerParams(vmem_limit_bytes=4 * 2**20),
     )(loss, head_grad, hidden_grad, gain_grad)
     return loss.reshape(128), head_grad, hidden_grad, gain_grad.reshape(16)
 

time: 88.8 us -> 80.5 us (0.907)
  Pallas kernels: 83.7 us -> 78.9 us
  local copies, waits for them, and re-layouts: 3.46 us -> 0 us
    unnamed x8 -> x0, local copies, waits for them, and re-layouts: 3.46 us -> none
    pallas_call x1, Pallas kernels: 79.8 us -> 77 us  [per_device(): pl.pallas_call(kernel, name='distill', out_shape=(vm((1, 128), F32), vm((...]
    pallas_call x1, Pallas kernels: 3.92 us -> 1.88 us  [per_device(): pl.pallas_call(store, name='store', out_shape=[jax.ShapeDtypeStruct(a.sha...]
where the time goes in v4:
time: 80.5 us; the launch traced here: 79.6 us
  Pallas kernels  78.9 us (98%)
    pallas_call x1, Pallas kernels, per_device(): pl.pallas_call(kernel, name='distill', out_shape=(vm((1, 128), F32), vm((...  77 us
    pallas_call x1, Pallas kernels, per_device(): pl.pallas_call(store, name='store', out_shape=[jax.ShapeDtypeStruct(a.sha...  1.88 us

profile of v4, /device:TPU:2, one launch (start us, length us, event | category | flops | bytes accessed | tf_op | source)
XLA Modules:
  0.0 79.6 jit_solution(1071709415795166570)
XLA Ops:
  0.6 77.0 %distill.1 = (f32[1,128]{1,0:T(1,128)S(1)}, bf16[2048,896]{1,0:T(8,128)(2,1)S(1)}, bf16[16,512]{1,0:T(8,128)(2,1)S(1)}, f32[1,16]{1,0:T(1,128)S(1)}) custom-call(bf16[1,128,4096]{2,1,0:T(8,128)(2,1)} %hs.1, bf16[1,4096,896]{2,1,0:T(8,128)(2,1)} %w_hbm.1, f32[2,4096]{1,0:T(2,128)} %gains_hbm.1, s32[1,128]{1,0:T(1,128)} %bitcast.3), custom_call_target="tpu_custom_call" | custom-call | flops 10000000000 | bytes 20000000 | tf_op jit(solution)/shard_map/distill/pallas_call | solution.py:714
  77.7 1.9 %store.1 = (f32[1,128]{1,0:T(1,128)}, bf16[2048,896]{1,0:T(8,128)(2,1)}, bf16[16,512]{1,0:T(8,128)(2,1)}, f32[1,16]{1,0:T(1,128)}) custom-call(f32[1,128]{1,0:T(1,128)S(1)} %get-tuple-element.12.loss, bf16[2048,896]{1,0:T(8,128)(2,1)S(1)} %get-tuple-element.13.head, bf16[16,512]{1,0:T(8,128)(2,1)S(1)} %get-tuple-element.14.hidden, ...), custom_call_target="tpu_custom_call" | custom-call | tf_op jit(solution)/shard_map/store/pallas_call | solution.py:731

commit v5 on v4

--- a/solution.py
+++ b/solution.py
@@ -14,7 +14,7 @@
 Y_SUB, Z_SUB = 512, 128
 Z_BASE = NY * Y_SUB
 X_BASE = Z_BASE + NZ * Z_SUB
-ROWS = 32
+ROWS = 128
 PEERS = [(0, 0, d) for d in (1, 2, 3)] + [(0, d, 0) for d in (1, 2, 3)] + [(d, 0, 0) for d in range(1, 8)]
 
 
@@ -32,9 +32,9 @@
     xg, nrm, w, w1h, n1h, n1t, z, zp, e_own, e_given, lg,
     info, info1, invb, labb, gains, label, xblk, ut,
     statc, st_send, st_recv, losses, colb, gainb,
-    ng, q1, q2, r1, s2, r2, s3, r3, rt_s, rt_r1, rt_r2, rt_r3, fin,
+    ng, q1, q2, r1, s2, r2, s3, r3, rt_s, rt_r, rt_other, fin,
     loc, xs_s, xs_r, ys_s, ys_r, zs_s, zs_r, in_s, in_r, pr_s, pr_r,
-    sa_s, sa_r, sz_s, sz_r, ab_s, ab_r, cz_s, cz_r,
+    sa_s, sa_r, sz_s, sz_r, ab_s, ab_r, cz_s, cz_r, rt_sem,
 ):
     g = lax.axis_index("grp")
     v = lax.axis_index("vocab")
@@ -82,17 +82,24 @@
         return pl.ds(pl.multiple_of(Z_BASE + at * Z_SUB, 128), Z_SUB)
 
     def x_copy(kind, d, to):
-        cols = (z_cols(zc), y_cols(yc, 0), y_cols(yc, 1), pl.ds(X_BASE, 1024))[kind]
+        cols = (z_cols(zc), y_cols(yc, 0), y_cols(yc, 1))[kind]
         at = s if to else lax.rem(s + NX - d, NX)
         dst = xg.at[at, :, cols]
         return remote(
-            hs.at[0, :, cols] if to else dst, dst, xs_s.at[kind, d - 1], xs_r.at[kind, d - 1], device(0, 0, d)
+            dst, dst, xs_s.at[kind, d - 1], xs_r.at[kind, d - 1], device(0, 0, d)
         )
+
+    def x_near(part, k, to):
+        d = 1 + 2 * k
+        cols = pl.ds(X_BASE + 512 * (k if part == 0 else 1 - k), 512)
+        at = s if to else lax.rem(s + NX - d, NX)
+        dst = xg.at[at, :, cols]
+        return remote(dst, dst, xs_s.at[3 + part, k], xs_r.at[3 + part, k], device(0, 0, d))
 
     def x_relay(k, to):
         d = 1 + 2 * k
         ref = xg.at[lax.rem(s + (NX - d if to else 2), NX), :, pl.ds(X_BASE + 512 * k, 512)]
-        return remote(ref, ref, xs_s.at[4, k], xs_r.at[4, k], device(0, 0, d))
+        return remote(ref, ref, xs_s.at[5, k], xs_r.at[5, k], device(0, 0, d))
 
     def info_copy(d, to):
         at = s if to else lax.rem(s + NX - d, NX)
@@ -101,8 +108,10 @@
     def x_start(kind):
         each(3, lambda i: x_copy(kind, i + 1, True).start())
 
+    load_x.wait()
     x_start(0)
     x_start(1)
+    x_start(2)
     load_w.start()
 
     half_w = pl.ds(0, 2048)
@@ -117,7 +126,6 @@
         w_copy().start()
         load_w1.start()
 
-    load_x.wait()
     load_g.wait()
     load_l.wait()
     total = jnp.zeros((128, 128), F32)
@@ -179,12 +187,15 @@
             y_relay(part, k, i + 1, True).start()
 
     each(3, forward_z)
-    x_start(2)
     each(3, lambda i: forward_y(0, i))
-    for k in range(2):
-        x_copy(3, 1 + 2 * k, True).start()
+    for part in range(2):
+        for k in range(2):
+            x_near(part, k, True).start()
     each(3, lambda i: forward_y(1, i))
     each(3, pass_z)
+    for k in range(2):
+        x_near(0, k, False).wait_recv()
+        x_relay(k, True).start()
     each(3, lambda i: pass_y(0, i))
 
     each(3, lambda i: info_copy(i + 1, False).wait_recv())
@@ -213,9 +224,6 @@
 
     accumulate(yc * Y_SUB, Y_SUB, first=True)
     each(3, lambda i: pass_y(1, i))
-    for k in range(2):
-        x_copy(3, 1 + 2 * k, False).wait_recv()
-        x_relay(k, True).start()
 
     def add_y(i):
         accumulate(lax.rem(yc + 1 + 2 * i, NY) * Y_SUB, Y_SUB)
@@ -237,6 +245,8 @@
 
     each(3, take_y)
     accumulate(lax.rem(yc + 2, NY) * Y_SUB, Y_SUB)
+    for k in range(2):
+        x_near(1, k, False).wait_recv()
     x_relay(0, False).wait_recv()
     accumulate(X_BASE, 512)
     x_relay(1, False).wait_recv()
@@ -418,22 +428,6 @@
     lg_trade.start()
     loss_trade.start()
 
-    def states_grad(h):
-        tokens = lg[pl.ds(pl.multiple_of(h * 256, 256), 256), :]
-
-        def tile(i):
-            rows = w1h[pl.ds(pl.multiple_of(i * 512, 512), 512), :]
-            product = lax.dot_general(rows, tokens, (((1,), (1,)), ((), ())), preferred_element_type=F32)
-            for k in range(2):
-                for y in range(NY):
-                    for x in range(NX):
-                        at = k * 256 + (y * NX + x) * 16
-                        a = x + (y - x) * h
-                        b = y + (x - y) * h
-                        ng[h, a, b, 2 * i + k] = product[at : at + 16].astype(BF16)
-
-        each(4, tile)
-
     def first(h):
         return s + (yc - s) * h
 
@@ -450,31 +444,53 @@
         src = ng.at[h, lax.rem(first(h) + d, 4), blocks] if part == 1 else q2.at[h, k]
         return remote(src, r1.at[h, k, blocks], *sems, to)
 
-    def at_copy(h, d):
-        to = device(0, d * h, d * (1 - h))
-        return remote(rt_s.at[h, 3], rt_r1.at[h, d - 1], ab_s.at[h, 2, d - 1], ab_r.at[h, 2, d - 1], to)
+    def rt_copy(step, d):
+        to = (device(d, 0, 0), device(0, 0, d), device(0, d, 0))[step]
+        slot = (0, 7, 10)[step] + d - 1
+        return remote(rt_s.at[step], rt_r.at[slot], rt_sem.at[0, slot], rt_sem.at[1, slot], to)
+
+    def start_rt(step):
+        each((7, 3, 3)[step], lambda i: rt_copy(step, i + 1).start())
+
+    def take_rt(step):
+        count, slot = ((7, 0), (3, 7), (3, 10))[step]
+        each(count, lambda i: rt_copy(step, i + 1).wait_recv())
+        total = rt_s[step]
+        for i in range(count):
+            total += rt_r[slot + i]
+        rt_s[step + 1] = total
+
+    rt_trade = remote(rt_s.at[3], rt_other, pr_s.at[6], pr_r.at[6], partner)
 
     def b_copy(h, d):
         to = device(0, d * (1 - h), d * h)
         return remote(s2.at[h, lax.rem(second(h) + d, 4)], r2.at[h, d - 1], ab_s.at[h, 3, d - 1], ab_r.at[h, 3, d - 1], to)
 
-    def bt_copy(h, d):
-        to = device(0, d * (1 - h), d * h)
-        return remote(rt_s.at[h, 0], rt_r2.at[h, d - 1], ab_s.at[h, 4, d - 1], ab_r.at[h, 4, d - 1], to)
-
     def c_copy(h, d):
         return remote(s3.at[h, lax.rem(zc + d, NZ)], r3.at[h, d - 1], cz_s.at[h, 0, d - 1], cz_r.at[h, 0, d - 1], device(d, 0, 0))
 
-    def ct_copy(h, d):
-        return remote(rt_s.at[h, 1], rt_r3.at[h, d - 1], cz_s.at[h, 1, d - 1], cz_r.at[h, 1, d - 1], device(d, 0, 0))
-
-    def start_a(h):
-        for part in range(2):
-            for k in range(2):
-                a_copy(h, k, part).start()
-
-    def start_at(h):
-        each(3, lambda i: at_copy(h, i + 1).start())
+    def states_grad(h):
+        tokens = lg[pl.ds(pl.multiple_of(h * 256, 256), 256), :]
+
+        def shard(a):
+            rows = []
+            for k in range(NZ):
+                for b in range(4):
+                    at = k * 256 + b * (64 - 48 * h) + a * (16 + 48 * h)
+                    rows.append(w1h[pl.ds(pl.multiple_of(at, 16), 16), :])
+            rows = jnp.concatenate(rows, axis=0)
+            product = lax.dot_general(rows, tokens, (((1,), (1,)), ((), ())), preferred_element_type=F32)
+            for k in range(NZ):
+                for b in range(4):
+                    ng[h, a, b, k] = product[(4 * k + b) * 16 : (4 * k + b) * 16 + 16].astype(BF16)
+
+        shard(lax.rem(first(h) + 2, 4))
+        for k in range(2):
+            a_copy(h, k, 0).start()
+        for k in range(2):
+            shard(lax.rem(first(h) + 1 + 2 * k, 4))
+            a_copy(h, k, 1).start()
+        shard(first(h))
 
     def pass_a(h):
         for k in range(2):
@@ -489,7 +505,6 @@
             a_copy(h, k, 2).start()
 
     def start_b(h):
-        each(3, lambda i: at_copy(h, i + 1).wait_recv())
         for k in range(2):
             a_copy(h, k, 1).wait_recv()
             a_copy(h, k, 2).wait_recv()
@@ -503,18 +518,15 @@
                 s2[h, b, k] = total.astype(BF16)
 
         each(4, add)
-        rt_s[h, 0] = rt_s[h, 3] + rt_r1[h, 0] + rt_r1[h, 1] + rt_r1[h, 2]
 
         def go(i):
             b_copy(h, i + 1).start()
-            bt_copy(h, i + 1).start()
 
         each(3, go)
 
     def start_c(h):
         def got(i):
             b_copy(h, i + 1).wait_recv()
-            bt_copy(h, i + 1).wait_recv()
 
         each(3, got)
         mine = second(h)
@@ -523,33 +535,25 @@
             for i in range(3):
                 total += r2[h, i, k].astype(F32)
             s3[h, k] = total.astype(BF16)
-        rt_s[h, 1] = rt_s[h, 0] + rt_r2[h, 0] + rt_r2[h, 1] + rt_r2[h, 2]
 
         def go(i):
             c_copy(h, i + 1).start()
-            ct_copy(h, i + 1).start()
 
         each(7, go)
 
     def finish(h):
         def got(i):
             c_copy(h, i + 1).wait_recv()
-            ct_copy(h, i + 1).wait_recv()
 
         each(7, got)
         total = s3[h, zc].astype(F32)
-        along = rt_s[h, 1]
         for i in range(7):
             total += r3[h, i].astype(F32)
-            along += rt_r3[h, i]
         fin[h] = total
-        rt_s[h, 2] = along
 
     states_grad(g)
-    start_a(g)
     lg_trade.wait_recv()
     states_grad(other)
-    start_a(other)
 
     def along(r):
         rows = pl.ds(pl.multiple_of(r * ROWS, ROWS), ROWS)
@@ -559,14 +563,10 @@
         statc[rows, :] = jnp.broadcast_to(total, (ROWS, 128))
 
     each(256 // ROWS, along)
-    rt_s[g, 3] = jnp.transpose(statc[...])[0:1]
-    rt_trade = remote(rt_s.at[g, 3], rt_s.at[g, 3], pr_s.at[6], pr_r.at[6], partner)
-    rt_trade.start()
-    start_at(g)
-    rt_trade.wait()
+    rt_s[0] = jnp.transpose(statc[...])[0:1]
+    start_rt(0)
     lg_trade.wait_send()
     loss_trade.wait()
-    start_at(other)
 
     def head_tile(i):
         rows = pl.ds(pl.multiple_of(i * 512, 512), 512)
@@ -580,10 +580,17 @@
 
     start_b(g)
     start_b(other)
+    take_rt(0)
+    start_rt(1)
     start_c(g)
     start_c(other)
+    take_rt(1)
+    start_rt(2)
+    take_rt(2)
+    rt_trade.start()
     finish(g)
     finish(other)
+    rt_trade.wait_recv()
 
     inv_row = jnp.concatenate([info1[i, 0:1] for i in range(4)], axis=1)
     mine16 = pl.ds(pl.multiple_of(lax.rem(vs, 8) * 16, 16), 16)
@@ -593,7 +600,7 @@
         cols = pl.ds(h * 256, 256)
         unit = ut[mine16, cols]
         grad = fin[h]
-        row_mean = rt_s[h, 2] * (SOFTEN_TEMP / 4096)
+        row_mean = jnp.where(g == h, rt_s[3], rt_other[...]) * (SOFTEN_TEMP / 4096)
         hidden = inv_row[:, h * 256 : h * 256 + 256] * (grad * gain16 - unit * row_mean)
         hidden_out[:, cols] = hidden.astype(BF16)
         gain_total += jnp.sum(grad * unit, axis=1, keepdims=True)
@@ -604,7 +611,8 @@
     for kind in range(3):
         each(3, lambda i, kind=kind: x_copy(kind, i + 1, True).wait_send())
     for k in range(2):
-        x_copy(3, 1 + 2 * k, True).wait_send()
+        for part in range(2):
+            x_near(part, k, True).wait_send()
         x_relay(k, True).wait_send()
 
     def sent_yz(i):
@@ -630,13 +638,10 @@
 
     def sent_ab(h):
         def one(i):
-            at_copy(h, i + 1).wait_send()
             b_copy(h, i + 1).wait_send()
-            bt_copy(h, i + 1).wait_send()
 
         def two(i):
             c_copy(h, i + 1).wait_send()
-            ct_copy(h, i + 1).wait_send()
 
         for part in range(3):
             for k in range(2):
@@ -645,6 +650,9 @@
         each(7, two)
 
     each(2, sent_ab)
+    for step, count in enumerate((7, 3, 3)):
+        each(count, lambda i, step=step: rt_copy(step, i + 1).wait_send())
+    rt_trade.wait_send()
 
 
 def store(loss, head, hidden, gain, loss_out, head_out, hidden_out, gain_out, sems):
@@ -693,13 +701,12 @@
         vm((2, 3, 8, 16, 256), BF16),
         vm((2, 8, 16, 256), BF16),
         vm((2, 7, 16, 256), BF16),
-        vm((2, 4, 1, 256), F32),
-        vm((2, 3, 1, 256), F32),
-        vm((2, 3, 1, 256), F32),
-        vm((2, 7, 1, 256), F32),
+        vm((4, 1, 256), F32),
+        vm((13, 1, 256), F32),
+        vm((1, 256), F32),
         vm((2, 16, 256), F32),
         dma((8,)),
-        dma((5, 3)), dma((5, 3)),
+        dma((6, 3)), dma((6, 3)),
         dma((2, 4, 3)), dma((2, 4, 3)),
         dma((8, 3)), dma((8, 3)),
         dma((3,)), dma((3,)),
@@ -708,6 +715,7 @@
         dma((7,)), dma((7,)),
         dma((2, 5, 3)), dma((2, 5, 3)),
         dma((2, 2, 7)), dma((2, 2, 7)),
+        dma((2, 13)),
     ]
     whole = pl.BlockSpec(memory_space=pltpu.HBM)
     vmem = pl.BlockSpec(memory_space=pltpu.VMEM)

time: 80.5 us -> 76.9 us (0.955)
  Pallas kernels: 78.9 us -> 75.5 us
    pallas_call x1, Pallas kernels: 77 us -> 73.6 us  [per_device(): pl.pallas_call(kernel, name='distill', out_shape=(vm((1, 128), F32), vm((...]
where the time goes in v5:
time: 76.9 us; the launch traced here: 76.2 us
  Pallas kernels  75.5 us (98%)
    pallas_call x1, Pallas kernels, per_device(): pl.pallas_call(kernel, name='distill', out_shape=(vm((1, 128), F32), vm((...  73.6 us
    pallas_call x1, Pallas kernels, per_device(): pl.pallas_call(store, name='store', out_shape=[jax.ShapeDtypeStruct(a.sha...  1.88 us

profile of v5, /device:TPU:2, one launch (start us, length us, event | category | flops | bytes accessed | tf_op | source)
XLA Modules:
  0.0 76.2 jit_solution(12715463187074681458)
XLA Ops:
  0.6 73.6 %distill.1 = (f32[1,128]{1,0:T(1,128)S(1)}, bf16[2048,896]{1,0:T(8,128)(2,1)S(1)}, bf16[16,512]{1,0:T(8,128)(2,1)S(1)}, f32[1,16]{1,0:T(1,128)S(1)}) custom-call(bf16[1,128,4096]{2,1,0:T(8,128)(2,1)} %hs.1, bf16[1,4096,896]{2,1,0:T(8,128)(2,1)} %w_hbm.1, f32[2,4096]{1,0:T(2,128)} %gains_hbm.1, s32[1,128]{1,0:T(1,128)} %bitcast.3), custom_call_target="tpu_custom_call" | custom-call | flops 10000000000 | bytes 20000000 | tf_op jit(solution)/shard_map/distill/pallas_call | solution.py:722
  74.3 1.9 %store.1 = (f32[1,128]{1,0:T(1,128)}, bf16[2048,896]{1,0:T(8,128)(2,1)}, bf16[16,512]{1,0:T(8,128)(2,1)}, f32[1,16]{1,0:T(1,128)}) custom-call(f32[1,128]{1,0:T(1,128)S(1)} %get-tuple-element.12.loss, bf16[2048,896]{1,0:T(8,128)(2,1)S(1)} %get-tuple-element.13.head, bf16[16,512]{1,0:T(8,128)(2,1)S(1)} %get-tuple-element.14.hidden, ...), custom_call_target="tpu_custom_call" | custom-call | tf_op jit(solution)/shard_map/store/pallas_call | solution.py:739

commit v6 on v5

--- a/solution.py
+++ b/solution.py
@@ -12,6 +12,8 @@
 F32, BF16 = jnp.float32, jnp.bfloat16
 NX, NY, NZ = 4, 4, 8
 Y_SUB, Z_SUB = 512, 128
+Y_PARTS = 4
+Y_PART = Y_SUB // Y_PARTS
 Z_BASE = NY * Y_SUB
 X_BASE = Z_BASE + NZ * Z_SUB
 ROWS = 128
@@ -73,16 +75,13 @@
     pl.semaphore_wait(barrier, len(PEERS) + 1)
 
     def y_cols(y, part):
-        return pl.ds(pl.multiple_of(y * Y_SUB + part * 256, 256), 256)
-
-    def y_half(y, part, k):
-        return pl.ds(pl.multiple_of(y * Y_SUB + part * 256 + k * 128, 128), 128)
+        return pl.ds(pl.multiple_of(y * Y_SUB + part * Y_PART, Y_PART), Y_PART)
 
     def z_cols(at):
         return pl.ds(pl.multiple_of(Z_BASE + at * Z_SUB, 128), Z_SUB)
 
     def x_copy(kind, d, to):
-        cols = (z_cols(zc), y_cols(yc, 0), y_cols(yc, 1))[kind]
+        cols = y_cols(yc, kind - 1) if kind else z_cols(zc)
         at = s if to else lax.rem(s + NX - d, NX)
         dst = xg.at[at, :, cols]
         return remote(
@@ -94,12 +93,12 @@
         cols = pl.ds(X_BASE + 512 * (k if part == 0 else 1 - k), 512)
         at = s if to else lax.rem(s + NX - d, NX)
         dst = xg.at[at, :, cols]
-        return remote(dst, dst, xs_s.at[3 + part, k], xs_r.at[3 + part, k], device(0, 0, d))
+        return remote(dst, dst, xs_s.at[1 + Y_PARTS + part, k], xs_r.at[1 + Y_PARTS + part, k], device(0, 0, d))
 
     def x_relay(k, to):
         d = 1 + 2 * k
         ref = xg.at[lax.rem(s + (NX - d if to else 2), NX), :, pl.ds(X_BASE + 512 * k, 512)]
-        return remote(ref, ref, xs_s.at[5, k], xs_r.at[5, k], device(0, 0, d))
+        return remote(ref, ref, xs_s.at[3 + Y_PARTS, k], xs_r.at[3 + Y_PARTS, k], device(0, 0, d))
 
     def info_copy(d, to):
         at = s if to else lax.rem(s + NX - d, NX)
@@ -109,9 +108,8 @@
         each(3, lambda i: x_copy(kind, i + 1, True).start())
 
     load_x.wait()
-    x_start(0)
-    x_start(1)
-    x_start(2)
+    for kind in range(1 + Y_PARTS):
+        x_start(kind)
     load_w.start()
 
     half_w = pl.ds(0, 2048)
@@ -150,7 +148,7 @@
     def y_relay(part, k, d, to):
         shard = lax.rem(s + NX - d, NX)
         dy = 1 + 2 * k
-        ref = xg.at[shard, :, y_half(lax.rem(yc + (NY - dy if to else 2), NY), part, k)]
+        ref = xg.at[shard, pl.ds(64 * k, 64), y_cols(lax.rem(yc + (NY - dy if to else 2), NY), part)]
         return remote(ref, ref, ys_s.at[part, 2 + k, d - 1], ys_r.at[part, 2 + k, d - 1], device(0, dy, 0))
 
     def z_copy(slot, d, to):
@@ -191,12 +189,14 @@
     for part in range(2):
         for k in range(2):
             x_near(part, k, True).start()
-    each(3, lambda i: forward_y(1, i))
+    for part in range(1, Y_PARTS):
+        each(3, lambda i, part=part: forward_y(part, i))
     each(3, pass_z)
     for k in range(2):
         x_near(0, k, False).wait_recv()
         x_relay(k, True).start()
-    each(3, lambda i: pass_y(0, i))
+    for part in range(Y_PARTS // 2):
+        each(3, lambda i, part=part: pass_y(part, i))
 
     each(3, lambda i: info_copy(i + 1, False).wait_recv())
     tall = jnp.transpose(jnp.concatenate([info[i] for i in range(4)] + [jnp.zeros((96, 128), F32)], axis=0))
@@ -223,7 +223,8 @@
             z[...] += product
 
     accumulate(yc * Y_SUB, Y_SUB, first=True)
-    each(3, lambda i: pass_y(1, i))
+    for part in range(Y_PARTS // 2, Y_PARTS):
+        each(3, lambda i, part=part: pass_y(part, i))
 
     def add_y(i):
         accumulate(lax.rem(yc + 1 + 2 * i, NY) * Y_SUB, Y_SUB)
@@ -239,7 +240,7 @@
     accumulate(Z_BASE + 512, 512)
 
     def take_y(i):
-        for part in range(2):
+        for part in range(Y_PARTS):
             for k in range(2):
                 y_relay(part, k, i + 1, False).wait_recv()
 
@@ -363,6 +364,25 @@
         sems = (sz_s.at[d - 1], sz_r.at[d - 1]) if axis == 2 else (sa_s.at[axis, d - 1], sa_r.at[axis, d - 1])
         return remote(st_send.at[axis], st_recv.at[axis * 3 + d - 1], *sems, to)
 
+    def sent_gather():
+        for kind in range(1 + Y_PARTS):
+            each(3, lambda i, kind=kind: x_copy(kind, i + 1, True).wait_send())
+        for k in range(2):
+            for part in range(2):
+                x_near(part, k, True).wait_send()
+            x_relay(k, True).wait_send()
+
+        def sent_yz(i):
+            info_copy(i + 1, True).wait_send()
+            for part in range(Y_PARTS):
+                for k in range(2):
+                    y_copy(part, k, i + 1, True).wait_send()
+                    y_relay(part, k, i + 1, True).wait_send()
+            for slot in range(8):
+                z_copy(slot, i + 1, True).wait_send()
+
+        each(3, sent_yz)
+
     def prepare():
         @pl.when(g == 0)
         def _():
@@ -401,6 +421,8 @@
         if axis:
             st_send[axis] = merged
         each(count, lambda i, axis=axis: st_copy(axis, i + 1).start())
+        if axis == 1:
+            sent_gather()
         if axis == 2:
             prepare()
         each(count, lambda i, axis=axis: st_copy(axis, i + 1).wait_recv())
@@ -577,13 +599,30 @@
     head_tile(2)
     pass_a(other)
     head_tile(3)
+    for axis, count in ((0, 3), (1, 3), (2, 7)):
+        each(count, lambda i, axis=axis: st_copy(axis, i + 1).wait_send())
+    @pl.when(g == 1)
+    def _():
+        w_copy().wait_send()
+        xblk_copy.wait_send()
+        info_pair.wait_send()
+        n1_copy.wait_send()
 
     start_b(g)
     start_b(other)
+
+    def sent_a(h):
+        for part in range(3):
+            for k in range(2):
+                a_copy(h, k, part).wait_send()
+
+    each(2, sent_a)
     take_rt(0)
     start_rt(1)
     start_c(g)
     start_c(other)
+    each(2, lambda h: each(3, lambda i: b_copy(h, i + 1).wait_send()))
+    each(7, lambda i: rt_copy(0, i + 1).wait_send())
     take_rt(1)
     start_rt(2)
     take_rt(2)
@@ -608,52 +647,10 @@
     gain_out[...] = jnp.transpose(wide)[0:1, 0:16]
     loss_out[...] = losses[lax.div(s, 2), :, pl.ds(pl.multiple_of(lax.rem(s, 2) * 128, 128), 128)]
 
-    for kind in range(3):
-        each(3, lambda i, kind=kind: x_copy(kind, i + 1, True).wait_send())
-    for k in range(2):
-        for part in range(2):
-            x_near(part, k, True).wait_send()
-        x_relay(k, True).wait_send()
-
-    def sent_yz(i):
-        info_copy(i + 1, True).wait_send()
-        for part in range(2):
-            for k in range(2):
-                y_copy(part, k, i + 1, True).wait_send()
-                y_relay(part, k, i + 1, True).wait_send()
-        for slot in range(8):
-            z_copy(slot, i + 1, True).wait_send()
-
-    each(3, sent_yz)
-
-    @pl.when(g == 1)
-    def _():
-        w_copy().wait_send()
-        xblk_copy.wait_send()
-        info_pair.wait_send()
-        n1_copy.wait_send()
-
-    for axis, count in ((0, 3), (1, 3), (2, 7)):
-        each(count, lambda i, axis=axis: st_copy(axis, i + 1).wait_send())
-
-    def sent_ab(h):
-        def one(i):
-            b_copy(h, i + 1).wait_send()
-
-        def two(i):
-            c_copy(h, i + 1).wait_send()
-
-        for part in range(3):
-            for k in range(2):
-                a_copy(h, k, part).wait_send()
-        each(3, one)
-        each(7, two)
-
-    each(2, sent_ab)
-    for step, count in enumerate((7, 3, 3)):
-        each(count, lambda i, step=step: rt_copy(step, i + 1).wait_send())
+    each(2, lambda h: each(7, lambda i: c_copy(h, i + 1).wait_send()))
+    for step in (1, 2):
+        each(3, lambda i, step=step: rt_copy(step, i + 1).wait_send())
     rt_trade.wait_send()
-
 
 def store(loss, head, hidden, gain, loss_out, head_out, hidden_out, gain_out, sems):
     pairs = ((head, head_out), (hidden, hidden_out), (loss, loss_out), (gain, gain_out))
@@ -706,8 +703,8 @@
         vm((1, 256), F32),
         vm((2, 16, 256), F32),
         dma((8,)),
-        dma((6, 3)), dma((6, 3)),
-        dma((2, 4, 3)), dma((2, 4, 3)),
+        dma((4 + Y_PARTS, 3)), dma((4 + Y_PARTS, 3)),
+        dma((Y_PARTS, 4, 3)), dma((Y_PARTS, 4, 3)),
         dma((8, 3)), dma((8, 3)),
         dma((3,)), dma((3,)),
         dma((9,)), dma((9,)),

time: 76.9 us -> 76.2 us (level)
  no operation moved by 1% of the time
where the time goes in v6:
time: 76.2 us; the launch traced here: 76.1 us
  Pallas kernels  75.5 us (99%)
    pallas_call x1, Pallas kernels, per_device(): pl.pallas_call(kernel, name='distill', out_shape=(vm((1, 128), F32), vm((...  73.6 us
    pallas_call x1, Pallas kernels, per_device(): pl.pallas_call(store, name='store', out_shape=[jax.ShapeDtypeStruct(a.sha...  1.88 us

profile of v6, /device:TPU:2, one launch (start us, length us, event | category | flops | bytes accessed | tf_op | source)
XLA Modules:
  0.0 76.1 jit_solution(13108991425812479186)
XLA Ops:
  0.6 73.6 %distill.1 = (f32[1,128]{1,0:T(1,128)S(1)}, bf16[2048,896]{1,0:T(8,128)(2,1)S(1)}, bf16[16,512]{1,0:T(8,128)(2,1)S(1)}, f32[1,16]{1,0:T(1,128)S(1)}) custom-call(bf16[1,128,4096]{2,1,0:T(8,128)(2,1)} %hs.1, bf16[1,4096,896]{2,1,0:T(8,128)(2,1)} %w_hbm.1, f32[2,4096]{1,0:T(2,128)} %gains_hbm.1, s32[1,128]{1,0:T(1,128)} %bitcast.3), custom_call_target="tpu_custom_call" | custom-call | flops 10000000000 | bytes 20000000 | tf_op jit(solution)/shard_map/distill/pallas_call | solution.py:719
  74.3 1.9 %store.1 = (f32[1,128]{1,0:T(1,128)}, bf16[2048,896]{1,0:T(8,128)(2,1)}, bf16[16,512]{1,0:T(8,128)(2,1)}, f32[1,16]{1,0:T(1,128)}) custom-call(f32[1,128]{1,0:T(1,128)S(1)} %get-tuple-element.12.loss, bf16[2048,896]{1,0:T(8,128)(2,1)S(1)} %get-tuple-element.13.head, bf16[16,512]{1,0:T(8,128)(2,1)S(1)} %get-tuple-element.14.hidden, ...), custom_call_target="tpu_custom_call" | custom-call | tf_op jit(solution)/shard_map/store/pallas_call | solution.py:736
